TPU v7x, 32 devices: a whole 2x2x4 slice. The times are simulated.
32 devices in a mesh: dp: 8 (over y, x, core), tm: 4 (over z).
Axes of the slice: x: 2, y: 2, z: 4, core: 2. Of those that a mesh axis runs over, the one named last changes fastest.
Arguments:
- clips_x: bfloat16 [2, 16, 4, 8, 8, 512], P(None, 'dp', 'tm'), may hold values from -6 to 6
- frames: int32 [2, 16], P(None, 'dp'), may hold values from 8 to 32, as said below
- labels: int32 [2, 16], P(None, 'dp'), may hold values from 0 to 399
- spatial_weight: float32 [512, 2, 9, 1152], P(('dp', 'tm'))
- temporal_weight: float32 [512, 2, 3, 1152], P(('dp', 'tm'))
- head_weight: float32 [512, 400], P(('dp', 'tm'))
- affine: float32 [2, 2, 1664], replicated
- head_bias: float32 [400], replicated, may hold values from -2 to 2
- spatial_first: float32 [512, 2, 9, 1152], P(('dp', 'tm'))
- spatial_second: float32 [512, 2, 9, 1152], P(('dp', 'tm')), as said below
- temporal_first: float32 [512, 2, 3, 1152], P(('dp', 'tm'))
- temporal_second: float32 [512, 2, 3, 1152], P(('dp', 'tm')), as said below
- head_first: float32 [512, 400], P(('dp', 'tm'))
- head_second: float32 [512, 400], P(('dp', 'tm')), as said below
- affine_first: float32 [2, 2, 1664], replicated
- affine_second: float32 [2, 2, 1664], replicated, as said below
- bias_first: float32 [400], replicated
- bias_second: float32 [400], replicated, as said below
Outputs:
- loss_sum: float32 [], replicated
- new_spatial_first: float32 [512, 2, 9, 1152], P(('dp', 'tm'))
- new_spatial_second: float32 [512, 2, 9, 1152], P(('dp', 'tm'))
- new_spatial_weight: float32 [512, 2, 9, 1152], P(('dp', 'tm'))
- new_temporal_first: float32 [512, 2, 3, 1152], P(('dp', 'tm'))
- new_temporal_second: float32 [512, 2, 3, 1152], P(('dp', 'tm'))
- new_temporal_weight: float32 [512, 2, 3, 1152], P(('dp', 'tm'))
- new_head_first: float32 [512, 400], P(('dp', 'tm'))
- new_head_second: float32 [512, 400], P(('dp', 'tm'))
- new_head_weight: float32 [512, 400], P(('dp', 'tm'))
- new_affine_first: float32 [2, 2, 1664], replicated
- new_affine_second: float32 [2, 2, 1664], replicated
- new_affine: float32 [2, 2, 1664], replicated
- new_bias_first: float32 [400], replicated
- new_bias_second: float32 [400], replicated
- new_head_bias: float32 [400], replicated
- norms: float32 [2, 5], replicated
Inputs may be any that keep to these rules, and one draw needn't show every extreme that they name: `frames`: each value is 8, 16 or 32; in every aligned block of 2 clips of one micro-batch at least one clip has 32. `spatial_second`: entries are positive. `temporal_second`: entries are positive. `head_second`: entries are positive. `affine_second`: entries are positive. `bias_second`: entries are positive.
All inputs are finite; a program needn't handle non-finite values.
Results may differ from a plain program's by a relative error of at most 0.014.
Values may be sent and summed in bfloat16 or wider, within the bound.
No kernel may reach another device: no remote copies, remote signals or barrier semaphores. Data moves between devices by JAX's collectives and lax.ppermute only.
A program may use at most 192 MiB of HBM per device.

v0:
```python
import functools

import jax
import jax.numpy as jnp
from jax import lax
from jax.experimental import pallas as pl
from jax.experimental.pallas import tpu as pltpu
from jax.sharding import Mesh
from jax.sharding import PartitionSpec as P

STEP = 5
EPS_NORM = 1e-05
EPS_ADAM = 1e-06
BETA_ONE = 0.5
BETA_TWO = 0.5
DECAY = 0.01
RATE = 0.3
RATE_SMALL = 0.1

F32 = jnp.float32
BF = jnp.bfloat16
LANES = 128
SPACE, TIME = 9, 3
ALL = ("yy", "s", "u", "tm")
DATA = ("yy", "tm")
MB = 1 << 20


def whole():
    return pl.BlockSpec(memory_space=pltpu.VMEM)


def anywhere():
    return pl.BlockSpec(memory_space=pl.ANY)


def smem():
    return pl.BlockSpec(memory_space=pltpu.SMEM)


def dot(a, b):
    return jnp.dot(a, b, preferred_element_type=F32)


def dot_nt(a, b):
    return lax.dot_general(a, b, (((1,), (1,)), ((), ())), preferred_element_type=F32)


class Dims:
    def __init__(self, clips, frames, height, width, channels, mid, rows, ny, nz):
        self.clips, self.frames, self.height, self.width = clips, frames, height, width
        self.channels, self.mid, self.rows, self.ny, self.nz = channels, mid, rows, ny, nz
        self.line = width * clips
        self.plane = height * self.line
        self.cells = frames * self.plane
        tiles = mid // LANES
        self.half = (tiles + 1) // 2 * LANES
        self.groups = ny * nz
        self.pieces = rows % 16 == 0 and ny == 2

    def row_base(self, yy, s, u, z):
        return (((yy * 2 + s) * 2 + u) * self.nz + z) * self.rows


class Weight:
    def __init__(self, kind, arrays, first, taps):
        self.kind, self.arrays, self.first, self.taps = kind, arrays, first, taps

    def part(self, first, taps):
        return Weight(self.kind, self.arrays, self.first + first, taps)

    def copies_needed(self, d):
        return 1 if self.kind == "natural" else 4 * d.groups

    def scratch(self, d):
        return [
            pltpu.VMEM((self.taps, d.channels, d.half), BF),
            pltpu.SemaphoreType.DMA((self.copies_needed(d),)),
        ]

    def places(self, d, ids):
        s, u, yy, z = (ids[i] for i in range(4))
        for urel in range(2):
            for i in range(d.groups):
                for srel in range(2):
                    if self.kind == "ring":
                        yrel, k = i // d.nz, i % d.nz
                        row = d.row_base(
                            yrel ^ yy, srel ^ s, urel ^ u, lax.rem(z + (d.nz - k), d.nz)
                        )
                        yield urel * d.groups + i, (srel,), row
                    else:
                        row = d.row_base(i // d.nz, srel ^ s, urel ^ u, i % d.nz)
                        yield urel, (i, srel), row

    def start(self, d, ids, refs, scratch, sems):
        taps = pl.ds(self.first, self.taps)
        copies = []
        if self.kind == "natural":
            copies.append(pltpu.make_async_copy(refs[0].at[taps], scratch, sems.at[0]))
        else:
            for operand, index, row in self.places(d, ids):
                copies.append(
                    pltpu.make_async_copy(
                        refs[operand].at[(*index, taps)],
                        scratch.at[:, pl.ds(pl.multiple_of(row, 16), d.rows), :],
                        sems.at[len(copies)],
                    )
                )
        for copy in copies:
            copy.start()
        return copies


def space_scratch(d, width):
    return pltpu.VMEM((3, d.frames, (d.height + 2) * d.line, width), BF)


def time_scratch(d, width):
    return pltpu.VMEM(((d.frames + 2) * d.plane, width), BF)


def fill_space(d, pad, values):
    cells, width = values.shape
    place = lax.broadcasted_iota(jnp.int32, (cells, width), 0)
    column = lax.rem(lax.div(place, d.clips), d.width)
    edge = jnp.zeros((3, d.frames, d.line, width), BF)
    pad[:, :, 0 : d.line, :] = edge
    pad[:, :, d.line + d.plane :, :] = edge
    left = jnp.where(column > 0, pltpu.roll(values, d.clips, 0), 0.0)
    right = jnp.where(column < d.width - 1, pltpu.roll(values, cells - d.clips, 0), 0.0)
    for j, moved in enumerate((left, values, right)):
        pad[j, :, d.line : d.line + d.plane, :] = moved.astype(BF).reshape(
            d.frames, d.plane, width
        )


def space_window(d, pad, i, j):
    start = pl.multiple_of(i * d.line, d.line)
    block = pad[j, :, pl.ds(start, d.plane), :]
    return block.reshape(d.cells, block.shape[-1])


def fill_time(d, pad, values):
    width = values.shape[1]
    edge = jnp.zeros((d.plane, width), BF)
    pad[0 : d.plane, :] = edge
    pad[d.plane + d.cells :, :] = edge
    pad[d.plane : d.plane + d.cells, :] = values


def time_window(d, pad, k):
    return pad[pl.ds(pl.multiple_of(k * d.plane, d.plane), d.cells), :]


def sums_of(first, second, extra=None):
    width = first.shape[1]
    rows = [jnp.sum(first, axis=0, keepdims=True), jnp.sum(second, axis=0, keepdims=True)]
    if extra is not None:
        rows.append(extra)
    rows.append(jnp.zeros((8 - len(rows), width), F32))
    return jnp.concatenate(rows, axis=0)


def coefs_of(total, count, gains):
    average = total[0:1] / count
    scale = lax.rsqrt(total[1:2] / count - average * average + EPS_NORM)
    return jnp.concatenate(
        [average, scale, gains[0:2], jnp.zeros((4, total.shape[1]), F32)], axis=0
    )


def normed_of(values, coef):
    return (values - coef[0:1]) * coef[1:2]


def act_slope(pre):
    sigma = jax.nn.sigmoid(pre)
    return sigma * (1.0 + pre * (1.0 - sigma))


def norm_back(grad_pre, normed, coef, total, count, mask):
    scale = coef[2:3] * coef[1:2]
    return mask * (scale * (grad_pre - (total[0:1] + normed * total[1:2]) / count))


def conv_space_into(d, acc, pad, weight):
    acc[...] = jnp.zeros_like(acc)

    @pl.loop(0, SPACE)
    def _(k):
        window = space_window(d, pad, lax.div(k, 3), lax.rem(k, 3))
        acc[...] += dot(window, weight[k])


def first_space_kernel(d, w, *refs):
    ids, *refs = refs
    w_refs, refs = refs[: len(w.arrays)], refs[len(w.arrays) :]
    x, mask, s_out, sums_out, weight, sems, pad = refs
    copies = w.start(d, ids, w_refs, weight, sems)
    fill_space(d, pad, x[...].astype(F32))
    for copy in copies:
        copy.wait()
    conv_space_into(d, s_out, pad, weight)
    m = mask[...]
    values = s_out[...]
    count = jnp.sum(m, axis=0, keepdims=True) + jnp.zeros((1, d.half), F32)
    sums_out[...] = sums_of(values * m, values * values * m, count)


def second_space_kernel(d, w, *refs):
    ids, *refs = refs
    w_refs, refs = refs[: len(w.arrays)], refs[len(w.arrays) :]
    q, va, vb, count, gains, mask, a_out, coef_out, s_out, sums_out, weight, sems, pad = refs
    copies = w.start(d, ids, w_refs, weight, sems)
    m = mask[...]
    coef = coefs_of(va[...] + vb[...], count[...], gains[...])
    coef_out[...] = coef
    pre = coef[2:3] * normed_of(q[...].astype(F32), coef) + coef[3:4]
    act = jax.nn.silu(pre) * m
    a_out[...] = act.astype(BF)
    fill_space(d, pad, act)
    for copy in copies:
        copy.wait()
    conv_space_into(d, s_out, pad, weight)
    values = s_out[...]
    sums_out[...] = sums_of(values * m, values * values * m)


def time_kernel(d, w, *refs):
    ids, *refs = refs
    w_refs, refs = refs[: len(w.arrays)], refs[len(w.arrays) :]
    s, va, vb, count, gains, mask, a_out, q_out, coef_out, weight, sems, pad = refs
    copies = w.start(d, ids, w_refs, weight, sems)
    coef = coefs_of(va[...] + vb[...], count[...], gains[...])
    coef_out[...] = coef
    pre = coef[2:3] * normed_of(s[...], coef) + coef[3:4]
    act = (jax.nn.silu(pre) * mask[...]).astype(BF)
    a_out[...] = act
    fill_time(d, pad, act)
    for copy in copies:
        copy.wait()
    total = dot_nt(time_window(d, pad, 0), weight[0])
    for k in range(1, TIME):
        total = total + dot_nt(time_window(d, pad, k), weight[k])
    q_out[...] = total.astype(BF)


def join_kernel(qa, qb, mask, q_out, sums_out):
    total = (qa[...].astype(F32) + qb[...].astype(F32)).astype(BF)
    q_out[...] = total
    values = total.astype(F32)
    m = mask[...]
    sums_out[...] = sums_of(values * m, values * values * m)


def head_kernel(d, w, denominator, classes, *refs):
    ids, *refs = refs
    w_refs, refs = refs[: len(w.arrays)], refs[len(w.arrays) :]
    q, va, vb, count, gains, mask, x, bias, clip_info, labels, *refs = refs
    coef_out, grad_out, sums_out, head, sems = refs
    copies = w.start(d, ids, w_refs, head, sems)
    m = mask[...]
    coef = coefs_of(va[...] + vb[...], count[...], gains[...])
    coef_out[...] = coef
    normed = normed_of(q[...].astype(F32), coef)
    pre = coef[2:3] * normed + coef[3:4] + x[...].astype(F32)
    sigma = jax.nn.sigmoid(pre)
    y = pre * sigma * m
    folded = jnp.sum(y.reshape(d.cells // 8, 8, d.channels), axis=0)
    step = d.clips
    total = folded
    for k in range(1, 8 // step):
        total = total + pltpu.roll(folded, k * step, 0)
    inverse = 1.0 / clip_info[:, 0:1]
    pooled = total * inverse
    pooled_bf = pooled.astype(BF)
    for copy in copies:
        copy.wait()
    weight = head[0, :, : d.channels]
    logits = dot(pooled_bf, weight) + bias[...]
    largest = jnp.max(logits, axis=1, keepdims=True)
    shifted = jnp.exp(logits - largest)
    log_total = largest + jnp.log(jnp.sum(shifted, axis=1, keepdims=True))
    lane = lax.broadcasted_iota(jnp.int32, logits.shape, 1)
    onehot = jnp.where(lane == labels[:, 0:1], 1.0, 0.0)
    inside = lane < classes
    kept = jnp.where(inside, logits, 0.0)
    loss = log_total - jnp.sum(kept * onehot, axis=1, keepdims=True)
    grad_logits = jnp.where(inside, (jnp.exp(logits - log_total) - onehot) / denominator, 0.0)
    grad_pooled = dot_nt(grad_logits.astype(BF), weight) * inverse
    grad_y = jnp.broadcast_to(grad_pooled[None], (d.cells // 8, 8, d.channels)).reshape(
        d.cells, d.channels
    )
    grad_pre = grad_y * m * (sigma * (1.0 + pre * (1.0 - sigma)))
    grad_out[...] = grad_pre
    sums_out[0:8, :] = sums_of(grad_pre, grad_pre * normed)
    carried = jnp.where(lane == classes, loss, grad_logits)
    sums_out[8:16, :] = jnp.concatenate(
        [
            pooled_bf.astype(F32)[0 : d.clips],
            carried[0 : d.clips],
            jnp.zeros((8 - 2 * d.clips, d.channels), F32),
        ],
        axis=0,
    )


def time_back_kernel(d, w, *refs):
    ids, *refs = refs
    w_refs, refs = refs[: len(w.arrays)], refs[len(w.arrays) :]
    grad_two, q, coef_two, va, vb, count, mask, s, coef_one, *refs = refs
    gq_out, grad_out, sums_out, tot_out, weight, sems, pad = refs
    copies = w.start(d, ids, w_refs, weight, sems)
    m = mask[...]
    total = va[...] + vb[...]
    tot_out[...] = total
    coef = coef_two[...]
    normed = normed_of(q[...].astype(F32), coef)
    grad_q = norm_back(grad_two[...], normed, coef, total, count[...], m).astype(BF)
    gq_out[...] = grad_q
    fill_time(d, pad, grad_q)
    for copy in copies:
        copy.wait()
    grad = dot(time_window(d, pad, TIME - 1), weight[0])
    for k in range(1, TIME):
        grad = grad + dot(time_window(d, pad, TIME - 1 - k), weight[k])
    grad = grad.astype(BF).astype(F32)
    coef = coef_one[...]
    normed = normed_of(s[...], coef)
    pre = coef[2:3] * normed + coef[3:4]
    grad_pre = grad * m * act_slope(pre)
    grad_out[...] = grad_pre
    sums_out[...] = sums_of(grad_pre, grad_pre * normed)


def space_back_kernel(d, w, *refs):
    ids, *refs = refs
    w_refs, refs = refs[: len(w.arrays)], refs[len(w.arrays) :]
    grad_pre, s, coef_one, va, vb, count, mask, *refs = refs
    gs_out, ga_out, tot_out, weight, sems, pad, acc = refs
    copies = w.start(d, ids, w_refs, weight, sems)
    total = va[...] + vb[...]
    tot_out[...] = total
    coef = coef_one[...]
    normed = normed_of(s[...], coef)
    grad_s = norm_back(grad_pre[...], normed, coef, total, count[...], mask[...])
    gs_out[...] = grad_s.astype(BF)
    fill_space(d, pad, grad_s)
    for copy in copies:
        copy.wait()
    acc[...] = jnp.zeros_like(acc)

    @pl.loop(0, SPACE)
    def _(k):
        window = space_window(d, pad, 2 - lax.div(k, 3), 2 - lax.rem(k, 3))
        acc[...] += dot_nt(window, weight[k])

    ga_out[...] = acc[...].astype(BF)


def join_back_kernel(ga, gb, q, coef_two, mask, grad_out, sums_out):
    coef = coef_two[...]
    normed = normed_of(q[...].astype(F32), coef)
    pre = coef[2:3] * normed + coef[3:4]
    grad = ga[...].astype(F32) + gb[...].astype(F32)
    grad_pre = grad * mask[...] * act_slope(pre)
    grad_out[...] = grad_pre
    sums_out[...] = sums_of(grad_pre, grad_pre * normed)


def write_grad(d, w, ids, value, outs, held):
    if w.kind == "natural":
        outs[0][0] = value.astype(BF)
        return
    held[...] = value.astype(BF)
    for operand, index, row in w.places(d, ids):
        block = held[pl.ds(pl.multiple_of(row, 16), d.rows), :]
        outs[operand][(*index, 0)] = block


def time_grad_kernel(d, w, *refs):
    ids, grad_q, act, *refs = refs
    outs, (pad, turned, held) = refs[:-3], refs[-3:]
    k = pl.program_id(0)

    @pl.when(k == 0)
    def _():
        fill_time(d, pad, act[...])
        turned[...] = jnp.transpose(grad_q[...].astype(F32)).astype(BF)

    write_grad(d, w, ids, dot(turned[...], time_window(d, pad, k)), outs, held)


def space_grad_kernel(d, w, *refs):
    ids, a, grad_s, *refs = refs
    outs, (pad, turned, held) = refs[:-3], refs[-3:]
    k = pl.program_id(0)

    @pl.when(k == 0)
    def _():
        fill_space(d, pad, grad_s[...].astype(F32))
        turned[...] = jnp.transpose(a[...].astype(F32)).astype(BF)

    window = space_window(d, pad, 2 - lax.div(k, 3), 2 - lax.rem(k, 3))
    write_grad(d, w, ids, dot(turned[...], window), outs, held)


def last_space_grad_kernel(d, w, *refs):
    ids, a, grad_pre, s, coef_one, va, vb, count, mask, tot_out, *refs = refs
    outs, (pad, turned, held) = refs[:-3], refs[-3:]
    k = pl.program_id(0)

    @pl.when(k == 0)
    def _():
        total = va[...] + vb[...]
        tot_out[...] = total
        coef = coef_one[...]
        normed = normed_of(s[...], coef)
        grad_s = norm_back(grad_pre[...], normed, coef, total, count[...], mask[...])
        fill_space(d, pad, grad_s)
        turned[...] = jnp.transpose(a[...].astype(F32)).astype(BF)

    window = space_window(d, pad, 2 - lax.div(k, 3), 2 - lax.rem(k, 3))
    write_grad(d, w, ids, dot(turned[...], window), outs, held)


def sds(shape, dtype=F32):
    return jax.ShapeDtypeStruct(shape, dtype)


def call(body, name, ins, outs, scratch, flops, megabytes=40):
    return pl.pallas_call(
        body,
        name=name,
        out_shape=outs,
        in_specs=[spec for spec, _ in ins],
        out_specs=[whole()] * len(outs),
        scratch_shapes=scratch,
        compiler_params=pltpu.CompilerParams(vmem_limit_bytes=megabytes * MB),
        cost_estimate=pl.CostEstimate(flops=flops, bytes_accessed=8 * MB, transcendentals=0),
    )(*[value for _, value in ins])


def w_ins(weight):
    return [(anywhere(), piece) for piece in weight.arrays]


def v_ins(*values):
    return [(whole(), value) for value in values]


def grad_call(d, body, name, kind, taps, ids, values, first_outs, scratch):
    if kind == "ring":
        shape, count = (2, taps, d.rows, d.half), 2 * d.groups
        spec = pl.BlockSpec((2, 1, d.rows, d.half), lambda k: (0, k, 0, 0))
    elif kind == "all":
        shape, count = (d.groups, 2, taps, d.rows, d.half), 2
        spec = pl.BlockSpec((d.groups, 2, 1, d.rows, d.half), lambda k: (0, 0, k, 0, 0))
    else:
        shape, count = (taps, d.channels, d.half), 1
        spec = pl.BlockSpec((1, d.channels, d.half), lambda k: (k, 0, 0))
    fixed = [pl.BlockSpec(out.shape, lambda k: (0, 0)) for out in first_outs]
    outs = pl.pallas_call(
        functools.partial(body, d, Weight(kind, (), 0, 1)),
        name=name,
        grid=(taps,),
        out_shape=list(first_outs) + [sds(shape, BF)] * count,
        in_specs=[smem()] + [whole()] * len(values),
        out_specs=fixed + [spec] * count,
        scratch_shapes=scratch
        + [pltpu.VMEM((d.channels, d.cells), BF), pltpu.VMEM((d.channels, d.half), BF)],
        compiler_params=pltpu.CompilerParams(vmem_limit_bytes=40 * MB),
        cost_estimate=pl.CostEstimate(
            flops=2 * taps * d.cells * d.channels * d.half,
            bytes_accessed=8 * MB,
            transcendentals=0,
        ),
    )(ids, *values)
    return outs[: len(first_outs)], outs[len(first_outs) :]


def swap(value, axis, distance=1):
    size = lax.axis_size(axis)
    return lax.ppermute(value, axis, [(i, i ^ distance) for i in range(size)])


def data_hops():
    hops = []
    for axis in DATA:
        distance = 1
        while distance < lax.axis_size(axis):
            hops.append((axis, distance))
            distance *= 2
    return hops


def data_sums(values):
    hops = data_hops()
    for axis, distance in hops[:-1]:
        values = values + swap(values, axis, distance)
    return values, swap(values, *hops[-1])


def data_sums_gather(values):
    hops = data_hops()
    for axis, distance in hops[:-1]:
        other = swap(values, axis, distance)
        values = jnp.concatenate([values[:8] + other[:8], values[8:], other[8:]], axis=0)
    other = swap(values, *hops[-1])
    return values[:8], other[:8], jnp.concatenate([values[8:], other[8:]], axis=0)


def pick(index, first, second):
    return jnp.where(index == 0, first, second)


def after(value, *earlier):
    return lax.optimization_barrier((value, *earlier))[0]


def turn(value):
    size = lax.axis_size("tm")
    return lax.ppermute(value, "tm", [(i, (i + 1) % size) for i in range(size)])


def gather_ring(both):
    held, across = [both], [swap(both, "yy")]
    for _ in range(lax.axis_size("tm") - 1):
        held.append(turn(held[-1]))
        across.append(swap(held[-1], "yy"))
    own = held + across
    return Weight("ring", own + [swap(block, "u") for block in own], 0, both.shape[1])


def gather_all(d, s, u, both, *earlier):
    own = lax.all_gather(both, DATA, axis=0, tiled=False)
    own = after(own, *earlier) if earlier else own
    sibling = swap(own, "u")
    taps = both.shape[1]
    if d.pieces:
        return Weight("all", (own, sibling), 0, taps)
    parts = jnp.stack([own, sibling]).reshape(2, d.ny, d.nz, 2, taps, d.rows, d.half)
    parts = jnp.where(u == 0, parts, parts[::-1])
    parts = jnp.where(s == 0, parts, parts[:, :, :, ::-1])
    natural = parts.transpose(4, 1, 3, 0, 2, 5, 6).reshape(taps, d.channels, d.half)
    return Weight("natural", (natural,), 0, taps)


def added(*values):
    total = values[0].astype(F32)
    for value in values[1:]:
        total = total + value.astype(F32)
    return total.astype(BF)


def reduce_ring(d, outs):
    n = d.nz
    keep, send = outs[: d.groups], outs[d.groups :]
    moving = None
    for k in list(range(1, n)) + [0]:
        across = swap(added(keep[n + k], swap(send[n + k], "u")), "yy")
        terms = [keep[k], swap(send[k], "u"), across]
        if moving is not None:
            terms.append(turn(moving))
        moving = added(*terms)
    return moving


def reduce_all(d, s, u, kind, out_lists):
    if kind == "all":
        both = jnp.concatenate(
            [added(keep, swap(send, "u")) for keep, send in out_lists], axis=2
        )
    else:
        natural = jnp.concatenate([outs[0] for outs in out_lists], axis=0)
        taps = natural.shape[0]
        parts = natural.reshape(taps, d.ny, 2, 2, d.nz, d.rows, d.half)
        parts = parts.transpose(3, 1, 4, 2, 0, 5, 6)
        parts = jnp.where(u == 0, parts, parts[::-1])
        parts = jnp.where(s == 0, parts, parts[:, :, :, ::-1])
        keep, send = parts.reshape(2, d.groups, 2, taps, d.rows, d.half)
        both = added(keep, swap(send, "u"))
    return lax.psum_scatter(both, DATA, scatter_dimension=0, tiled=False)


def own_rows(d, s, mine):
    other = swap(mine[1], "s")
    first = pick(s, mine[0], other)
    second = pick(s, other, mine[0])
    return jnp.concatenate([first, second[..., : d.mid - d.half]], axis=-1).astype(F32)


def halves(d, values):
    fill = [(0, 0)] * (values.ndim - 1) + [(0, 2 * d.half - d.mid)]
    return values[..., : d.half], jnp.pad(values[..., d.half :], fill)


def rows_of(gain, shift):
    return jnp.concatenate(
        [gain[None], shift[None], jnp.zeros((6, gain.shape[0]), F32)], axis=0
    )


def adam_part(weight, gradient, moment_one, moment_two, decay):
    new_one = BETA_ONE * moment_one + (1.0 - BETA_ONE) * gradient
    new_two = BETA_TWO * moment_two + (1.0 - BETA_TWO) * gradient * gradient
    direction = (
        new_one / (1.0 - BETA_ONE**STEP) / (jnp.sqrt(new_two / (1.0 - BETA_TWO**STEP)) + EPS_ADAM)
        + decay * weight
    )
    return (new_one, new_two, direction)


def on_device(
    clips_x,
    frames,
    labels,
    spatial_weight,
    temporal_weight,
    head_weight,
    affine,
    head_bias,
    spatial_first,
    spatial_second,
    temporal_first,
    temporal_second,
    head_first,
    head_second,
    affine_first,
    affine_second,
    bias_first,
    bias_second,
):
    s, u, z, yy = (lax.axis_index(axis) for axis in ("s", "u", "tm", "yy"))
    ny, nz = lax.axis_size("yy"), lax.axis_size("tm")
    micro, clips, _, height, width, channels = clips_x.shape
    mid = spatial_weight.shape[3]
    rows = spatial_weight.shape[0]
    classes = head_weight.shape[1]
    d = Dims(clips, nz, height, width, channels, mid, rows, ny, nz)
    assert nz == 4 and micro == 2
    ids = jnp.stack([s, u, yy, z]).astype(jnp.int32)
    denominator = micro * clips * 4 * ny

    def prepared(weight, l):
        moved = weight[:, l].astype(BF).transpose(1, 0, 2)
        return halves(d, moved)

    head_slot = jnp.pad(head_weight.astype(BF), ((0, 0), (0, d.half - classes)))[None]
    space_parts = [prepared(spatial_weight, l) for l in range(2)]
    time_parts = [prepared(temporal_weight, l) for l in range(2)]

    def paired(parts):
        first = jnp.concatenate([part[0] for part in parts], axis=0)
        second = jnp.concatenate([part[1] for part in parts], axis=0)
        own = pick(s, first, second)
        return jnp.stack([own, swap(pick(s, second, first), "s")])

    early = paired([space_parts[0], time_parts[0]])
    late = paired([space_parts[1], time_parts[1], (head_slot, head_slot)])
    if d.pieces:
        early_w = gather_ring(early)
    else:
        early_w = gather_all(d, s, u, early)

    def by_index(index, mine, other):
        return jnp.stack([pick(index, mine, other), pick(index, other, mine)])

    kept = pick(u, clips_x[0], clips_x[1])
    other = swap(pick(u, clips_x[1], clips_x[0]), "u")
    pair = by_index(u, kept, other)
    four = by_index(s, pair, swap(pair, "s"))
    four = four.reshape(nz, clips, height * width, channels)
    clip_all = lax.all_to_all(four, "tm", split_axis=0, concat_axis=0, tiled=True)
    x = clip_all.reshape(nz, clips, height * width, channels)
    x = x.transpose(0, 2, 1, 3).reshape(d.cells, channels)

    info = jnp.stack([frames, labels]).transpose(1, 0, 2)
    kept_info = pick(u, info[0], info[1])
    pair_info = by_index(u, kept_info, swap(pick(u, info[1], info[0]), "u"))
    four_info = by_index(s, pair_info, swap(pair_info, "s")).reshape(nz, 2, clips)
    mine_info = lax.dynamic_index_in_dim(four_info, z, 0, keepdims=False)
    my_frames, my_labels = mine_info[0], mine_info[1]
    valid = (jnp.arange(nz, dtype=jnp.int32)[:, None] * 8 < my_frames[None, :]).astype(F32)
    mask = jnp.broadcast_to(valid[:, None, :], (nz, height * width, clips)).reshape(d.cells, 1)
    divisor = (my_frames // 8).astype(F32) * (height * width)
    clip_info = jnp.broadcast_to(jnp.tile(divisor, 8 // clips)[:, None], (8, LANES))
    label_rows = jnp.broadcast_to(jnp.tile(my_labels, 8 // clips)[:, None], (8, LANES))
    bias_row = jnp.full((1, channels), -1e30, F32).at[0, :classes].set(head_bias)

    gains_one, gains_two = [], []
    for l in range(2):
        low, high = halves(d, affine[l, :, :mid])
        mine = pick(s, low, high)
        gains_one.append(rows_of(mine[0], mine[1]))
        gains_two.append(rows_of(affine[l, 0, mid:], affine[l, 1, mid:]))

    wide, narrow = (d.cells, d.half), (d.cells, channels)
    space_flops = 2 * d.cells * SPACE * channels * d.half
    time_flops = 2 * d.cells * TIME * channels * d.half

    space_w = [early_w.part(0, SPACE), None]
    time_w = [early_w.part(SPACE, TIME), None]

    def space_first(x_bf):
        return call(
            functools.partial(first_space_kernel, d, space_w[0]),
            "space0",
            [(smem(), ids)] + w_ins(space_w[0]) + v_ins(x_bf, mask),
            [sds(wide), sds((8, d.half))],
            space_w[0].scratch(d) + [space_scratch(d, channels)],
            space_flops,
        )

    def space_next(q, va, vb, count):
        return call(
            functools.partial(second_space_kernel, d, space_w[1]),
            "space1",
            [(smem(), ids)] + w_ins(space_w[1]) + v_ins(q, va, vb, count, gains_two[0], mask),
            [sds(narrow, BF), sds((8, channels)), sds(wide), sds((8, d.half))],
            space_w[1].scratch(d) + [space_scratch(d, channels)],
            space_flops,
        )

    def time_next(l, s_value, va, vb, count):
        return call(
            functools.partial(time_kernel, d, time_w[l]),
            f"time{l}",
            [(smem(), ids)] + w_ins(time_w[l]) + v_ins(s_value, va, vb, count, gains_one[l], mask),
            [sds(wide, BF), sds(narrow, BF), sds((8, d.half))],
            time_w[l].scratch(d) + [time_scratch(d, d.half)],
            time_flops,
        )

    def joined(q_part):
        return call(
            join_kernel,
            "join",
            v_ins(q_part, swap(q_part, "s"), mask),
            [sds(narrow, BF), sds((8, channels))],
            [],
            d.cells * channels,
        )

    s0, sums = space_first(x)
    va, vb = data_sums(sums)
    count = va[2:3, 0:1] + vb[2:3, 0:1]
    late_w = gather_all(d, s, u, late, va)
    space_w[1] = late_w.part(0, SPACE)
    time_w[1] = late_w.part(SPACE, TIME)
    head_w = late_w.part(SPACE + TIME, 1)
    act0, q_part, coef_one0 = time_next(0, s0, va, vb, count)
    q0, sums = joined(q_part)
    va, vb = data_sums(sums)
    a_mid, coef_two0, s1, sums = space_next(q0, va, vb, count)
    va, vb = data_sums(sums)
    act1, q_part, coef_one1 = time_next(1, s1, va, vb, count)
    q1, sums = joined(q_part)
    va, vb = data_sums(sums)
    coef_two1, grad_two, sums = call(
        functools.partial(head_kernel, d, head_w, float(denominator), classes),
        "head",
        [(smem(), ids)]
        + w_ins(head_w)
        + v_ins(q1, va, vb, count, gains_two[1], mask, x, bias_row, clip_info, label_rows),
        [sds((8, channels)), sds(narrow), sds((16, channels))],
        head_w.scratch(d),
        4 * d.cells * channels,
    )
    va, vb, carried = data_sums_gather(sums)

    def time_back(l, grad, q, coef_two, va, vb, s_value, coef_one):
        return call(
            functools.partial(time_back_kernel, d, time_w[l]),
            f"time_back{l}",
            [(smem(), ids)]
            + w_ins(time_w[l])
            + v_ins(grad, q, coef_two, va, vb, count, mask, s_value, coef_one),
            [sds(narrow, BF), sds(wide), sds((8, d.half)), sds((8, channels))],
            time_w[l].scratch(d) + [time_scratch(d, channels)],
            time_flops,
        )

    late_kind = "all" if d.pieces else "natural"
    early_kind = "ring" if d.pieces else "natural"

    def time_grad(l, grad_q, act):
        return grad_call(
            d,
            time_grad_kernel,
            f"time_grad{l}",
            late_kind if l else early_kind,
            TIME,
            ids,
            (grad_q, act),
            [],
            [time_scratch(d, d.half)],
        )[1]

    grad_q1, grad_one, sums, tot_two1 = time_back(
        1, grad_two, q1, coef_two1, va, vb, s1, coef_one1
    )
    va, vb = data_sums(sums)
    time_outs1 = time_grad(1, grad_q1, act1)
    grad_s1, ga_part, tot_one1 = call(
        functools.partial(space_back_kernel, d, space_w[1]),
        "space_back",
        [(smem(), ids)] + w_ins(space_w[1]) + v_ins(grad_one, s1, coef_one1, va, vb, count, mask),
        [sds(wide, BF), sds(narrow, BF), sds((8, d.half))],
        space_w[1].scratch(d)
        + [space_scratch(d, d.half), pltpu.VMEM((d.cells, channels), F32)],
        space_flops,
    )
    ga_other = swap(ga_part, "s")
    _, space_outs1 = grad_call(
        d,
        space_grad_kernel,
        "space_grad1",
        late_kind,
        SPACE,
        ids,
        (a_mid, grad_s1),
        [],
        [space_scratch(d, d.half)],
    )
    grad_two, sums = call(
        join_back_kernel,
        "join_back",
        v_ins(ga_part, after(ga_other, *space_outs1), q0, coef_two0, mask),
        [sds(narrow), sds((8, channels))],
        [],
        4 * d.cells * channels,
    )
    va, vb = data_sums(sums)
    grad_q0, grad_one, sums, tot_two0 = time_back(
        0, grad_two, q0, coef_two0, va, vb, s0, coef_one0
    )
    va, vb = data_sums(sums)
    time_outs0 = time_grad(0, grad_q0, act0)
    (tot_one0,), space_outs0 = grad_call(
        d,
        last_space_grad_kernel,
        "space_grad0",
        early_kind,
        SPACE,
        ids,
        (x, grad_one, s0, coef_one0, va, vb, count, mask),
        [sds((8, d.half))],
        [space_scratch(d, d.half)],
    )

    late_sum = reduce_all(d, s, u, late_kind, [space_outs1, time_outs1])
    late_sum = own_rows(d, s, after(late_sum, *space_outs0))
    if d.pieces:
        early_sum = reduce_ring(
            d, [jnp.concatenate(pair, axis=1) for pair in zip(space_outs0, time_outs0)]
        )
    else:
        early_sum = reduce_all(d, s, u, early_kind, [space_outs0, time_outs0])
    early_sum = own_rows(d, s, early_sum)

    carried = jnp.concatenate([carried, swap(carried, "u")], axis=0).reshape(-1, 8, channels)
    pooled_all = carried[:, :clips].reshape(-1, channels)
    logit_all = carried[:, clips : 2 * clips].reshape(-1, channels)
    loss_sum = jnp.sum(logit_all[:, classes])
    logit_all = logit_all[:, :classes]
    bias_grad = jnp.sum(logit_all, axis=0)
    base = d.row_base(yy, s, u, z)
    pooled_mine = lax.dynamic_slice_in_dim(pooled_all, base, rows, 1)
    head_grad = lax.dot_general(
        pooled_mine.astype(BF),
        logit_all.astype(BF),
        (((0,), (0,)), ((), ())),
        preferred_element_type=F32,
    )

    ones = jnp.stack([tot_one0[:2], tot_one1[:2]])
    twos = jnp.stack([tot_two0[:2], tot_two1[:2]])
    small = jnp.concatenate([ones, twos], axis=-1)
    small = small + swap(small, "u")
    ones, twos = small[..., : d.half], small[..., d.half :]
    ones_other = swap(ones, "s")
    low, high = pick(s, ones, ones_other), pick(s, ones_other, ones)
    both = jnp.concatenate([low, high[..., : mid - d.half], twos], axis=-1)
    affine_grad = jnp.stack([both[:, 1], both[:, 0]], axis=1)

    def step(weight, first, second, gradients):
        return [
            (moved[0],) + adam_part(moved[0], gradient, moved[1], moved[2], DECAY)
            for l, gradient in enumerate(gradients)
            for moved in [[v[:, l].transpose(1, 0, 2) for v in (weight, first, second)]]
        ]

    def joined_units(parts):
        return jnp.stack(parts).transpose(2, 0, 1, 3)

    space_steps = step(
        spatial_weight, spatial_first, spatial_second, (early_sum[:SPACE], late_sum[:SPACE])
    )
    time_steps = step(
        temporal_weight, temporal_first, temporal_second, (early_sum[SPACE:], late_sum[SPACE:])
    )
    head_one, head_two, head_dir = adam_part(head_weight, head_grad, head_first, head_second, DECAY)
    affine_one, affine_two, affine_dir = adam_part(
        affine, affine_grad, affine_first, affine_second, 0.0
    )
    bias_one, bias_two, bias_dir = adam_part(head_bias, bias_grad, bias_first, bias_second, 0.0)

    steps = space_steps + time_steps
    dir_squares = [jnp.sum(part[3] * part[3]) for part in steps] + [jnp.sum(head_dir * head_dir)]
    weight_squares = [jnp.sum(part[0] * part[0]) for part in steps]
    weight_squares.append(jnp.sum(head_weight * head_weight))
    both_squares = jnp.stack([jnp.stack(weight_squares), jnp.stack(dir_squares)])
    padded = jnp.pad(both_squares, ((0, 6), (0, LANES - 5)))
    padded = padded + swap(padded, "u")
    padded = padded + swap(padded, "s")
    padded = sum(data_sums(padded))
    norms = jnp.sqrt(padded[:2, :5])
    trust = norms[0] / norms[1]
    new = [part[0] - RATE * trust[i] * part[3] for i, part in enumerate(steps)]
    space_one, space_two = (joined_units([part[i] for part in space_steps]) for i in (1, 2))
    time_one, time_two = (joined_units([part[i] for part in time_steps]) for i in (1, 2))
    new_space, new_time = joined_units(new[:2]), joined_units(new[2:])
    new_head = head_weight - RATE * trust[4] * head_dir
    new_affine = affine - RATE_SMALL * affine_dir
    new_bias = head_bias - RATE_SMALL * bias_dir
    return (
        loss_sum,
        space_one,
        space_two,
        new_space,
        time_one,
        time_two,
        new_time,
        head_one,
        head_two,
        new_head,
        affine_one,
        affine_two,
        new_affine,
        bias_one,
        bias_two,
        new_bias,
        norms,
    )


def solution(mesh):
    dp, tm = mesh.shape["dp"], mesh.shape["tm"]
    fine = Mesh(mesh.devices.reshape(dp // 4, 2, 2, tm), ALL)
    dp_axes = ("yy", "s", "u")
    owner = P(ALL)
    return jax.shard_map(
        on_device,
        mesh=fine,
        in_specs=(
            P(None, dp_axes, "tm"),
            P(None, dp_axes),
            P(None, dp_axes),
            owner,
            owner,
            owner,
            P(),
            P(),
            owner,
            owner,
            owner,
            owner,
            owner,
            owner,
            P(),
            P(),
            P(),
            P(),
        ),
        out_specs=(P(),) + (owner,) * 9 + (P(),) * 7,
        check_vma=False,
    )
```

profile of v0, /device:TPU:0, one launch (start us, length us, event | category | flops | bytes accessed | tf_op | source)
XLA Modules:
  0.0 517.2 jit_solution(13200648380035800233)
XLA Ops:
  15.9 6.3 %collective-permute-done = bf16[13,16,640]{2,1,0:T(8,128)(2,1)S(1)} collective-permute-done((bf16[13,16,640]{2,1,0:T(8,128)(2,1)S(1)}, bf16[13,16,640]{2,1,0:T(8,128)(2,1)S(1)}, u32[]{:S(2)}, u32[]{:S(2)}) %collective-permute-start) | collective-permute-done | bytes 266272 | tf_op jit(solution)/shard_map/ppermute | solution.py:485
  25.3 5.3 %collective-permute-done.1 = bf16[12,16,640]{2,1,0:T(8,128)(2,1)S(1)} collective-permute-done((bf16[12,16,640]{2,1,0:T(8,128)(2,1)S(1)}, bf16[12,16,640]{2,1,0:T(8,128)(2,1)S(1)}, u32[]{:S(2)}, u32[]{:S(2)}) %collective-permute-start.1) | collective-permute-done | bytes 245792 | tf_op jit(solution)/shard_map/ppermute | solution.py:485
  32.9 20.2 %collective-permute-done.2.refs_2_ = bf16[2,12,16,640]{3,2,1,0:T(8,128)(2,1)S(1)} collective-permute-done((bf16[2,12,16,640]{3,2,1,0:T(8,128)(2,1)S(1)}, bf16[2,12,16,640]{3,2,1,0:T(8,128)(2,1)S(1)}, u32[]{:S(2)}, u32[]{:S(2)}) %collective-permute-start.2) | collective-permute-done | bytes 491552 | tf_op jit(solution)/shard_map/ppermute | solution.py:524
  53.1 7.4 %collective-permute-start.3 = (bf16[2,12,16,640]{3,2,1,0:T(8,128)(2,1)S(1)}, bf16[2,12,16,640]{3,2,1,0:T(8,128)(2,1)S(1)}, u32[]{:S(2)}, u32[]{:S(2)}) collective-permute-start(bf16[2,12,16,640]{3,2,1,0:T(8,128)(2,1)S(1)} %collective-permute-done.2.refs_2_), channel_id=1, source_target_pairs={{0,1},{1,2},{2,3},{3,0},{4,5},{5,6},{6,7},{7,4},{8,9},{9,10},{10,1... | collective-permute-start | bytes 1474568 | tf_op jit(solution)/shard_map/ppermute | solution.py:524
  63.8 9.1 %collective-permute-done.3.refs_3_ = bf16[2,12,16,640]{3,2,1,0:T(8,128)(2,1)S(1)} collective-permute-done((bf16[2,12,16,640]{3,2,1,0:T(8,128)(2,1)S(1)}, bf16[2,12,16,640]{3,2,1,0:T(8,128)(2,1)S(1)}, u32[]{:S(2)}, u32[]{:S(2)}) %collective-permute-start.3) | collective-permute-done | bytes 491552 | tf_op jit(solution)/shard_map/ppermute | solution.py:524
  79.4 19.0 %collective-permute-done.4.refs_4_ = bf16[2,12,16,640]{3,2,1,0:T(8,128)(2,1)S(1)} collective-permute-done((bf16[2,12,16,640]{3,2,1,0:T(8,128)(2,1)S(1)}, bf16[2,12,16,640]{3,2,1,0:T(8,128)(2,1)S(1)}, u32[]{:S(2)}, u32[]{:S(2)}) %collective-permute-start.4) | collective-permute-done | bytes 491552 | tf_op jit(solution)/shard_map/ppermute | solution.py:524
  98.5 5.4 %collective-permute-start.8 = (bf16[2,12,16,640]{3,2,1,0:T(8,128)(2,1)S(1)}, bf16[2,12,16,640]{3,2,1,0:T(8,128)(2,1)}, u32[]{:S(2)}, u32[]{:S(2)}) collective-permute-start(bf16[2,12,16,640]{3,2,1,0:T(8,128)(2,1)S(1)} %collective-permute-done.4.refs_4_), channel_id=1, source_target_pairs={{0,16},{16,0},{1,17},{17,1},{2,18},{18,2},{3,19},{19,3},{4,20},{20... | collective-permute-start | bytes 1474568 | tf_op jit(solution)/shard_map/ppermute | solution.py:485
  110.5 7.6 %collective-permute-done.7.refs_7_ = bf16[2,12,16,640]{3,2,1,0:T(8,128)(2,1)} collective-permute-done((bf16[2,12,16,640]{3,2,1,0:T(8,128)(2,1)S(1)}, bf16[2,12,16,640]{3,2,1,0:T(8,128)(2,1)}, u32[]{:S(2)}, u32[]{:S(2)}) %collective-permute-start.7) | collective-permute-done | bytes 491552 | tf_op jit(solution)/shard_map/ppermute | solution.py:485
  118.1 7.5 %collective-permute-done.8.refs_8_ = bf16[2,12,16,640]{3,2,1,0:T(8,128)(2,1)} collective-permute-done((bf16[2,12,16,640]{3,2,1,0:T(8,128)(2,1)S(1)}, bf16[2,12,16,640]{3,2,1,0:T(8,128)(2,1)}, u32[]{:S(2)}, u32[]{:S(2)}) %collective-permute-start.8) | collective-permute-done | bytes 491552 | tf_op jit(solution)/shard_map/ppermute | solution.py:485
  133.1 8.8 %space0.1 = (f32[512,640]{1,0:T(8,128)S(1)}, f32[8,640]{1,0:T(8,128)S(1)}) custom-call(s32[4]{0:T(128)S(1)} %pad_add_fusion.2.refs_0_, bf16[2,12,16,640]{3,2,1,0:T(8,128)(2,1)S(1)} %pad_maximum_fusion.3.refs_1_, bf16[2,12,16,640]{3,2,1,0:T(8,128)(2,1)S(1)} %collective-permute-done.2.refs_2_, bf16[2,12,16,640]{3,2,1,0:T(8,128)(2,1)S(1)} %copy-done.16, ...), custom_call_target="tpu_custom_call" | custom-call | flops 3019898880 | bytes 8388608 | tf_op jit(solution)/shard_map/space0/pallas_call | solution.py:433
  141.9 5.2 %collective-permute-start.21 = (f32[8,640]{1,0:T(8,128)S(1)}, f32[8,640]{1,0:T(8,128)S(1)}, u32[]{:S(2)}, u32[]{:S(2)}) collective-permute-start(f32[8,640]{1,0:T(8,128)S(1)} %get-tuple-element.101), channel_id=1, source_target_pairs={{0,16},{16,0},{1,17},{17,1},{2,18},{18,2},{3,19},{19,3},{4,20},{20... | collective-permute-start | bytes 61448 | tf_op jit(solution)/shard_map/ppermute | solution.py:485
  168.8 13.3 %collective-permute-done.25.qb = bf16[512,512]{1,0:T(8,128)(2,1)S(1)} collective-permute-done((bf16[512,512]{1,0:T(8,128)(2,1)S(1)}, bf16[512,512]{1,0:T(8,128)(2,1)S(1)}, u32[]{:S(2)}, u32[]{:S(2)}) %collective-permute-start.25) | collective-permute-done | bytes 524320 | tf_op jit(solution)/shard_map/ppermute | solution.py:485
  194.7 8.0 %space1.1 = (bf16[512,512]{1,0:T(8,128)(2,1)S(1)}, f32[8,512]{1,0:T(8,128)S(1)}, f32[512,640]{1,0:T(8,128)S(1)}, f32[8,640]{1,0:T(8,128)S(1)}) custom-call(s32[4]{0:T(128)S(1)} %pad_add_fusion.2.refs_0_, bf16[8,2,13,16,640]{4,3,2,1,0:T(8,128)(2,1)S(1)} %bitcast.350, bf16[8,2,13,16,640]{4,3,2,1,0:T(8,128)(2,1)S(1)} %collective-permute-done.23.refs_2_, ...), custom_call_target="tpu_custom_call" | custom-call | flops 3019898880 | bytes 8388608 | tf_op jit(solution)/shard_map/space1/pallas_call | solution.py:433
  219.8 9.1 %collective-permute-done.32.qb = bf16[512,512]{1,0:T(8,128)(2,1)S(1)} collective-permute-done((bf16[512,512]{1,0:T(8,128)(2,1)S(1)}, bf16[512,512]{1,0:T(8,128)(2,1)S(1)}, u32[]{:S(2)}, u32[]{:S(2)}) %collective-permute-start.32) | collective-permute-done | bytes 524320 | tf_op jit(solution)/shard_map/ppermute | solution.py:485
  284.1 8.1 %space_back.1 = (bf16[512,640]{1,0:T(8,128)(2,1)S(1)}, bf16[512,512]{1,0:T(8,128)(2,1)S(1)}, f32[8,640]{1,0:T(8,128)S(1)}) custom-call(s32[4]{0:T(128)S(1)} %pad_add_fusion.2.refs_0_, bf16[8,2,13,16,640]{4,3,2,1,0:T(8,128)(2,1)S(1)} %bitcast.354, bf16[8,2,13,16,640]{4,3,2,1,0:T(8,128)(2,1)S(1)} %copy-done.2, f32[512,640]{1,0:T(8,128)S(1)} %get-tuple-element.116.refs_3_, ...), custom_call_target="tpu_custom_call" | custom-call | flops 3019898880 | bytes 8388608 | tf_op jit(solution)/shard_map/space_back/pallas_call | solution.py:433
  292.3 8.6 %space_grad1.1 = (bf16[8,2,9,16,640]{4,3,2,1,0:T(8,128)(2,1)S(1)}, bf16[8,2,9,16,640]{4,3,2,1,0:T(8,128)(2,1)}) custom-call(s32[4]{0:T(128)S(1)} %pad_add_fusion.2.refs_0_, bf16[512,512]{1,0:T(8,128)(2,1)S(1)} %copy-done.46, bf16[512,640]{1,0:T(8,128)(2,1)S(1)} %get-tuple-element.120.refs_2_), custom_call_target="tpu_custom_call" | custom-call | flops 3019898880 | bytes 8388608 | tf_op jit(solution)/shard_map/space_grad1/pallas_call | solution.py:464
  313.7 13.0 %collective-permute-done.43.gb = bf16[512,512]{1,0:T(8,128)(2,1)S(1)} collective-permute-done((bf16[512,512]{1,0:T(8,128)(2,1)S(1)}, bf16[512,512]{1,0:T(8,128)(2,1)S(1)}, u32[]{:S(2)}, u32[]{:S(2)}) %collective-permute-start.43) | collective-permute-done | bytes 524320 | tf_op jit(solution)/shard_map/ppermute | solution.py:485
  372.6 8.8 %space_grad0.1 = (f32[8,640]{1,0:T(8,128)S(1)}, bf16[2,9,16,640]{3,2,1,0:T(8,128)(2,1)S(1)}, bf16[2,9,16,640]{3,2,1,0:T(8,128)(2,1)S(1)}, bf16[2,9,16,640]{3,2,1...) custom-call(s32[4]{0:T(128)S(1)} %pad_add_fusion.2.refs_0_, ...), custom_call_target="tpu_custom_call" | custom-call | flops 3019898880 | bytes 8388608 | tf_op jit(solution)/shard_map/space_grad0/pallas_call | solution.py:464
  387.4 15.4 %collective-permute-done.61 = bf16[2,12,16,640]{3,2,1,0:T(8,128)(2,1)S(1)} collective-permute-done((bf16[2,12,16,640]{3,2,1,0:T(8,128)(2,1)S(1)}, bf16[2,12,16,640]{3,2,1,0:T(8,128)(2,1)S(1)}, u32[]{:S(2)}, u32[]{:S(2)}) %collective-permute-start.61) | collective-permute-done | bytes 491552 | tf_op jit(solution)/shard_map/ppermute | solution.py:485
  406.0 8.6 %collective-permute-done.58 = bf16[2,12,16,640]{3,2,1,0:T(8,128)(2,1)S(1)} collective-permute-done((bf16[2,12,16,640]{3,2,1,0:T(8,128)(2,1)S(1)}, bf16[2,12,16,640]{3,2,1,0:T(8,128)(2,1)S(1)}, u32[]{:S(2)}, u32[]{:S(2)}) %collective-permute-start.58) | collective-permute-done | bytes 491552 | tf_op jit(solution)/shard_map/ppermute | solution.py:485
  414.6 6.7 %collective-permute-done.62 = bf16[2,12,16,640]{3,2,1,0:T(8,128)(2,1)S(1)} collective-permute-done((bf16[2,12,16,640]{3,2,1,0:T(8,128)(2,1)S(1)}, bf16[2,12,16,640]{3,2,1,0:T(8,128)(2,1)S(1)}, u32[]{:S(2)}, u32[]{:S(2)}) %collective-permute-start.62) | collective-permute-done | bytes 491552 | tf_op jit(solution)/shard_map/ppermute | solution.py:524
  429.2 14.5 %collective-permute-done.63 = bf16[2,12,16,640]{3,2,1,0:T(8,128)(2,1)S(1)} collective-permute-done((bf16[2,12,16,640]{3,2,1,0:T(8,128)(2,1)S(1)}, bf16[2,12,16,640]{3,2,1,0:T(8,128)(2,1)S(1)}, u32[]{:S(2)}, u32[]{:S(2)}) %collective-permute-start.63) | collective-permute-done | bytes 491552 | tf_op jit(solution)/shard_map/ppermute | solution.py:524
  448.1 6.9 %collective-permute-done.64 = bf16[2,12,16,640]{3,2,1,0:T(8,128)(2,1)S(1)} collective-permute-done((bf16[2,12,16,640]{3,2,1,0:T(8,128)(2,1)S(1)}, bf16[2,12,16,640]{3,2,1,0:T(8,128)(2,1)S(1)}, u32[]{:S(2)}, u32[]{:S(2)}) %collective-permute-start.64) | collective-permute-done | bytes 491552 | tf_op jit(solution)/shard_map/ppermute | solution.py:524
  456.0 5.5 %collective-permute-done.65 = bf16[12,16,640]{2,1,0:T(8,128)(2,1)S(1)} collective-permute-done((bf16[12,16,640]{2,1,0:T(8,128)(2,1)S(1)}, bf16[12,16,640]{2,1,0:T(8,128)(2,1)S(1)}, u32[]{:S(2)}, u32[]{:S(2)}) %collective-permute-start.65) | collective-permute-done | bytes 245792 | tf_op jit(solution)/shard_map/ppermute | solution.py:485
  (515 shorter events, 268.5 us)
Async XLA Ops:
  7.2 145.4 %all-gather.3.cloned.1.call-start = ((), (), s32[]{:S(2)}) async-start(), calls=%async_computation.3 | async-start | bytes 4792320 | tf_op jit(solution)/shard_map/all_gather | solution.py:537
  30.7 22.4 %collective-permute-start.2 = (bf16[2,12,16,640]{3,2,1,0:T(8,128)(2,1)S(1)}, bf16[2,12,16,640]{3,2,1,0:T(8,128)(2,1)S(1)}, u32[]{:S(2)}, u32[]{:S(2)}) collective-permute-start(bf16[2,12,16,640]{3,2,1,0:T(8,128)(2,1)S(1)} %pad_maximum_fusion.3.refs_1_), channel_id=1, source_target_pairs={{0,1},{1,2},{2,3},{3,0},{4,5},{5,6},{6,7},{7,4},{8,9},{9,10},{10,1... | collective-permute-start | bytes 1474568 | tf_op jit(solution)/shard_map/ppermute | solution.py:524
  32.3 40.6 %collective-permute-start.19 = (s32[2,2]{1,0:T(2,128)S(1)}, s32[2,2]{1,0:T(2,128)S(1)}, u32[]{:S(2)}, u32[]{:S(2)}) collective-permute-start(s32[2,2]{1,0:T(2,128)S(1)} %bitcast.383), channel_id=1, source_target_pairs={{0,4},{4,0},{1,5},{5,1},{2,6},{6,2},{3,7},{7,3},{8,12},{12,8},{9,1... | collective-permute-start | bytes 56 | tf_op jit(solution)/shard_map/ppermute | solution.py:485
  32.4 28.2 %collective-permute-start.17 = (bf16[2,1,8,8,512]{4,3,2,0,1:T(8,128)(2,1)S(1)}, bf16[2,1,8,8,512]{4,3,2,0,1:T(8,128)(2,1)S(1)}, u32[]{:S(2)}, u32[]{:S(2)}) collective-permute-start(bf16[2,1,8,8,512]{4,3,2,0,1:T(8,128)(2,1)S(1)} %fusion.32), channel_id=1, source_target_pairs={{0,4},{4,0},{1,5},{5,1},{2,6},{6,2},{3,7},{7,3},{8,12},{12,8},{9,1... | collective-permute-start | bytes 393224 | tf_op jit(solution)/shard_map/ppermute | solution.py:485
  53.1 19.7 %collective-permute-start.3 = (bf16[2,12,16,640]{3,2,1,0:T(8,128)(2,1)S(1)}, bf16[2,12,16,640]{3,2,1,0:T(8,128)(2,1)S(1)}, u32[]{:S(2)}, u32[]{:S(2)}) collective-permute-start(bf16[2,12,16,640]{3,2,1,0:T(8,128)(2,1)S(1)} %collective-permute-done.2.refs_2_), channel_id=1, source_target_pairs={{0,1},{1,2},{2,3},{3,0},{4,5},{5,6},{6,7},{7,4},{8,9},{9,10},{10,1... | collective-permute-start | bytes 1474568 | tf_op jit(solution)/shard_map/ppermute | solution.py:524
  72.8 25.6 %collective-permute-start.4 = (bf16[2,12,16,640]{3,2,1,0:T(8,128)(2,1)S(1)}, bf16[2,12,16,640]{3,2,1,0:T(8,128)(2,1)S(1)}, u32[]{:S(2)}, u32[]{:S(2)}) collective-permute-start(bf16[2,12,16,640]{3,2,1,0:T(8,128)(2,1)S(1)} %collective-permute-done.3.refs_3_), channel_id=1, source_target_pairs={{0,1},{1,2},{2,3},{3,0},{4,5},{5,6},{6,7},{7,4},{8,9},{9,10},{10,1... | collective-permute-start | bytes 1474568 | tf_op jit(solution)/shard_map/ppermute | solution.py:524
  75.1 34.7 %collective-permute-start.6 = (bf16[2,12,16,640]{3,2,1,0:T(8,128)(2,1)S(1)}, bf16[2,12,16,640]{3,2,1,0:T(8,128)(2,1)}, u32[]{:S(2)}, u32[]{:S(2)}) collective-permute-start(bf16[2,12,16,640]{3,2,1,0:T(8,128)(2,1)S(1)} %collective-permute-done.2.refs_2_), channel_id=1, source_target_pairs={{0,16},{16,0},{1,17},{17,1},{2,18},{18,2},{3,19},{19,3},{4,20},{20... | collective-permute-start | bytes 1474568 | tf_op jit(solution)/shard_map/ppermute | solution.py:485
  77.4 32.5 %collective-permute-start.10 = (bf16[2,12,16,640]{3,2,1,0:T(8,128)(2,1)S(1)}, bf16[2,12,16,640]{3,2,1,0:T(8,128)(2,1)}, u32[]{:S(2)}, u32[]{:S(2)}) collective-permute-start(bf16[2,12,16,640]{3,2,1,0:T(8,128)(2,1)S(1)} %collective-permute-done.2.refs_2_), channel_id=1, source_target_pairs={{0,4},{4,0},{1,5},{5,1},{2,6},{6,2},{3,7},{7,3},{8,12},{12,8},{9,1... | collective-permute-start | bytes 1474568 | tf_op jit(solution)/shard_map/ppermute | solution.py:485
  77.5 33.0 %collective-permute-start.13 = (bf16[2,12,16,640]{3,2,1,0:T(8,128)(2,1)S(1)}, bf16[2,12,16,640]{3,2,1,0:T(8,128)(2,1)}, u32[]{:S(2)}, u32[]{:S(2)}) collective-permute-start(bf16[2,12,16,640]{3,2,1,0:T(8,128)(2,1)S(1)} %collective-permute-done.5.refs_5_), channel_id=1, source_target_pairs={{0,4},{4,0},{1,5},{5,1},{2,6},{6,2},{3,7},{7,3},{8,12},{12,8},{9,1... | collective-permute-start | bytes 1474568 | tf_op jit(solution)/shard_map/ppermute | solution.py:485
  78.0 40.2 %collective-permute-start.7 = (bf16[2,12,16,640]{3,2,1,0:T(8,128)(2,1)S(1)}, bf16[2,12,16,640]{3,2,1,0:T(8,128)(2,1)}, u32[]{:S(2)}, u32[]{:S(2)}) collective-permute-start(bf16[2,12,16,640]{3,2,1,0:T(8,128)(2,1)S(1)} %collective-permute-done.3.refs_3_), channel_id=1, source_target_pairs={{0,16},{16,0},{1,17},{17,1},{2,18},{18,2},{3,19},{19,3},{4,20},{20... | collective-permute-start | bytes 1474568 | tf_op jit(solution)/shard_map/ppermute | solution.py:485
  98.5 27.1 %collective-permute-start.8 = (bf16[2,12,16,640]{3,2,1,0:T(8,128)(2,1)S(1)}, bf16[2,12,16,640]{3,2,1,0:T(8,128)(2,1)}, u32[]{:S(2)}, u32[]{:S(2)}) collective-permute-start(bf16[2,12,16,640]{3,2,1,0:T(8,128)(2,1)S(1)} %collective-permute-done.4.refs_4_), channel_id=1, source_target_pairs={{0,16},{16,0},{1,17},{17,1},{2,18},{18,2},{3,19},{19,3},{4,20},{20... | collective-permute-start | bytes 1474568 | tf_op jit(solution)/shard_map/ppermute | solution.py:485
  105.3 20.5 %all-to-all-start = ((bf16[4,2,64,512]{3,1,2,0:T(2,128)(2,1)}), bf16[4,2,64,512]{3,1,2,0:T(2,128)(2,1)}, u32[]{:S(2)}, u32[]{:S(2)}) async-start(bf16[4,2,64,512]{3,1,2,0:T(2,128)(2,1)} %copy.115), calls=%async_computation | async-start | bytes 1048576 | tf_op jit(solution)/shard_map/all_to_all | solution.py:675
  109.4 355.9 %reduce-scatter.2.cloned.1.call-start = ((), (), s32[]{:S(2)}) async-start(), calls=%async_computation.2 | async-start | bytes 4423680 | tf_op jit(solution)/shard_map/reduce_scatter | solution.py:584
  152.6 42.0 %collective-permute-start.23 = (bf16[8,2,13,16,640]{4,3,2,1,0:T(8,128)(2,1)}, bf16[8,2,13,16,640]{4,3,2,1,0:T(8,128)(2,1)S(1)}, u32[]{:S(2)}, u32[]{:S(2)}) collective-permute-start(bf16[8,2,13,16,640]{4,3,2,1,0:T(8,128)(2,1)} %bitcast.347), channel_id=1, source_target_pairs={{0,4},{4,0},{1,5},{5,1},{2,6},{6,2},{3,7},{7,3},{8,12},{12,8},{9,1... | collective-permute-start | bytes 12779528 | tf_op jit(solution)/shard_map/ppermute | solution.py:485
  300.9 32.0 %collective-permute-start.66 = (bf16[8,2,9,16,640]{4,3,2,1,0:T(8,128)(2,1)}, bf16[8,2,9,16,640]{4,3,2,1,0:T(8,128)(2,1)}, u32[]{:S(2)}, u32[]{:S(2)}) collective-permute-start(bf16[8,2,9,16,640]{4,3,2,1,0:T(8,128)(2,1)} %get-tuple-element.122), channel_id=1, source_target_pairs={{0,4},{4,0},{1,5},{5,1},{2,6},{6,2},{3,7},{7,3},{8,12},{12,8},{9,1... | collective-permute-start | bytes 8847368 | tf_op jit(solution)/shard_map/ppermute | solution.py:485
  311.2 20.0 %collective-permute-start.67 = (bf16[8,2,3,16,640]{4,3,2,1,0:T(8,128)(2,1)}, bf16[8,2,3,16,640]{4,3,2,1,0:T(8,128)(2,1)}, u32[]{:S(2)}, u32[]{:S(2)}) collective-permute-start(bf16[8,2,3,16,640]{4,3,2,1,0:T(8,128)(2,1)} %get-tuple-element.167), channel_id=1, source_target_pairs={{0,4},{4,0},{1,5},{5,1},{2,6},{6,2},{3,7},{7,3},{8,12},{12,8},{9,1... | collective-permute-start | bytes 2949128 | tf_op jit(solution)/shard_map/ppermute | solution.py:485
  313.5 24.8 %collective-permute-start.39 = (f32[64,512]{1,0:T(8,128)S(1)}, f32[64,512]{1,0:T(8,128)}, u32[]{:S(2)}, u32[]{:S(2)}) collective-permute-start(f32[64,512]{1,0:T(8,128)S(1)} %pad_maximum_fusion.17), channel_id=1, source_target_pairs={{0,4},{4,0},{1,5},{5,1},{2,6},{6,2},{3,7},{7,3},{8,12},{12,8},{9,1... | collective-permute-start | bytes 393224 | tf_op jit(solution)/shard_map/ppermute | solution.py:485
  381.6 41.6 %collective-permute-start.51 = (bf16[2,12,16,640]{3,2,1,0:T(8,128)(2,1)S(1)}, bf16[2,12,16,640]{3,2,1,0:T(8,128)(2,1)S(1)}, u32[]{:S(2)}, u32[]{:S(2)}) collective-permute-start(bf16[2,12,16,640]{3,2,1,0:T(8,128)(2,1)S(1)} %pad_maximum_fusion.5), channel_id=1, source_target_pairs={{0,4},{4,0},{1,5},{5,1},{2,6},{6,2},{3,7},{7,3},{8,12},{12,8},{9,1... | collective-permute-start | bytes 1474568 | tf_op jit(solution)/shard_map/ppermute | solution.py:485
  386.4 28.1 %collective-permute-start.58 = (bf16[2,12,16,640]{3,2,1,0:T(8,128)(2,1)S(1)}, bf16[2,12,16,640]{3,2,1,0:T(8,128)(2,1)S(1)}, u32[]{:S(2)}, u32[]{:S(2)}) collective-permute-start(bf16[2,12,16,640]{3,2,1,0:T(8,128)(2,1)S(1)} %add_convert_fusion.7), channel_id=1, source_target_pairs={{0,16},{16,0},{1,17},{17,1},{2,18},{18,2},{3,19},{19,3},{4,20},{20... | collective-permute-start | bytes 1474568 | tf_op jit(solution)/shard_map/ppermute | solution.py:485
  405.1 24.1 %collective-permute-start.55 = (bf16[2,12,16,640]{3,2,1,0:T(8,128)(2,1)S(1)}, bf16[2,12,16,640]{3,2,1,0:T(8,128)(2,1)S(1)}, u32[]{:S(2)}, u32[]{:S(2)}) collective-permute-start(bf16[2,12,16,640]{3,2,1,0:T(8,128)(2,1)S(1)} %add_convert_fusion.8), channel_id=1, source_target_pairs={{0,16},{16,0},{1,17},{17,1},{2,18},{18,2},{3,19},{19,3},{4,20},{20... | collective-permute-start | bytes 1474568 | tf_op jit(solution)/shard_map/ppermute | solution.py:485
  421.5 22.1 %collective-permute-start.63 = (bf16[2,12,16,640]{3,2,1,0:T(8,128)(2,1)S(1)}, bf16[2,12,16,640]{3,2,1,0:T(8,128)(2,1)S(1)}, u32[]{:S(2)}, u32[]{:S(2)}) collective-permute-start(bf16[2,12,16,640]{3,2,1,0:T(8,128)(2,1)S(1)} %add_convert_fusion.4), channel_id=1, source_target_pairs={{0,1},{1,2},{2,3},{3,0},{4,5},{5,6},{6,7},{7,4},{8,9},{9,10},{10,1... | collective-permute-start | bytes 1474568 | tf_op jit(solution)/shard_map/ppermute | solution.py:524
  423.1 21.3 %collective-permute-start.74 = (f32[2,2,1152]{2,1,0:T(2,128)S(1)}, f32[2,2,1152]{2,1,0:T(2,128)S(1)}, u32[]{:S(2)}, u32[]{:S(2)}) collective-permute-start(f32[2,2,1152]{2,1,0:T(2,128)S(1)} %maximum_maximum_fusion), channel_id=1, source_target_pairs={{0,4},{4,0},{1,5},{5,1},{2,6},{6,2},{3,7},{7,3},{8,12},{12,8},{9,1... | collective-permute-start | bytes 55304 | tf_op jit(solution)/shard_map/ppermute | solution.py:485
  423.2 24.9 %collective-permute-start.50 = (bf16[2,12,16,640]{3,2,1,0:T(8,128)(2,1)S(1)}, bf16[2,12,16,640]{3,2,1,0:T(8,128)(2,1)S(1)}, u32[]{:S(2)}, u32[]{:S(2)}) collective-permute-start(bf16[2,12,16,640]{3,2,1,0:T(8,128)(2,1)S(1)} %pad_maximum_fusion.4), channel_id=1, source_target_pairs={{0,4},{4,0},{1,5},{5,1},{2,6},{6,2},{3,7},{7,3},{8,12},{12,8},{9,1... | collective-permute-start | bytes 1474568 | tf_op jit(solution)/shard_map/ppermute | solution.py:485
  423.9 24.2 %collective-permute-start.52 = (bf16[2,12,16,640]{3,2,1,0:T(8,128)(2,1)S(1)}, bf16[2,12,16,640]{3,2,1,0:T(8,128)(2,1)S(1)}, u32[]{:S(2)}, u32[]{:S(2)}) collective-permute-start(bf16[2,12,16,640]{3,2,1,0:T(8,128)(2,1)S(1)} %add_convert_fusion.9), channel_id=1, source_target_pairs={{0,16},{16,0},{1,17},{17,1},{2,18},{18,2},{3,19},{19,3},{4,20},{20... | collective-permute-start | bytes 1474568 | tf_op jit(solution)/shard_map/ppermute | solution.py:485
  (148 other events, 1206.3 us)
Sparse Core Ops, SparseCore 0:
  23.2 108.4 all-gather.2
  338.4 102.9 reduce-scatter.1
where the time goes:
time: 523 us; the launch traced here: 517 us
  waiting for transfers between devices  246 us (47%)
  starting transfers between devices  82.7 us (16%)
  Pallas kernels  70.3 us (13%)
  local copies, waits for them, and re-layouts  69.2 us (13%)
  other arithmetic  26.6 us (5%)
  between operations  20.4 us (4%)
    ppermute x70, waiting for transfers between devices, swap(): return lax.ppermute(value, axis, [(i, i ^ distance) for i in range(size)])  169 us
    ppermute x6, waiting for transfers between devices, turn(): return lax.ppermute(value, 'tm', [(i, (i + 1) % size) for i in range(size)])  76.4 us
    ppermute x70, starting transfers between devices, swap(): return lax.ppermute(value, axis, [(i, i ^ distance) for i in range(size)])  65.5 us
    pallas_call x11, Pallas kernels, call(): pl.pallas_call(body, name=name, out_shape=outs, in_specs=[spec for spec,...  46 us
    unnamed x197, local copies, waits for them, and re-layouts  40.6 us
    pallas_call x4, Pallas kernels, grad_call(): pl.pallas_call(functools.partial(body, d, Weight(kind, (), 0, 1)), name=n...  24.3 us
    ppermute x6, starting transfers between devices, turn(): return lax.ppermute(value, 'tm', [(i, (i + 1) % size) for i in range(size)])  12.7 us
  transfers between devices with their start and end apart: 79, of which 47 were waited for; matrix products, arithmetic and copies ran while one was open for 9% of the time, Pallas kernels for 7%

commit v1 on v0

--- a/solution.py
+++ b/solution.py
@@ -4,6 +4,7 @@
 import jax.numpy as jnp
 from jax import lax
 from jax.experimental import pallas as pl
+from jax.experimental.layout import Layout, with_layout_constraint
 from jax.experimental.pallas import tpu as pltpu
 from jax.sharding import Mesh
 from jax.sharding import PartitionSpec as P
@@ -30,8 +31,8 @@
     return pl.BlockSpec(memory_space=pltpu.VMEM)
 
 
-def anywhere():
-    return pl.BlockSpec(memory_space=pl.ANY)
+def in_hbm():
+    return pl.BlockSpec(memory_space=pltpu.HBM)
 
 
 def smem():
@@ -83,15 +84,21 @@
         for urel in range(2):
             for i in range(d.groups):
                 for srel in range(2):
-                    if self.kind == "ring":
+                    if self.kind in ("blocks", "ring"):
                         yrel, k = i // d.nz, i % d.nz
                         row = d.row_base(
                             yrel ^ yy, srel ^ s, urel ^ u, lax.rem(z + (d.nz - k), d.nz)
                         )
-                        yield urel * d.groups + i, (srel,), row
+                        if self.kind == "blocks":
+                            yield urel * d.groups + i, (srel,), row
+                        else:
+                            yield urel * 2 + yrel, (k, srel), row
                     else:
                         row = d.row_base(i // d.nz, srel ^ s, urel ^ u, i % d.nz)
-                        yield urel, (i, srel), row
+                        if self.kind == "all" or urel == 0:
+                            yield urel, (i, srel), row
+                        else:
+                            yield 1 + i // 2, (i % 2, srel), row
 
     def start(self, d, ids, refs, scratch, sems):
         taps = pl.ds(self.first, self.taps)
@@ -113,7 +120,7 @@
 
 
 def space_scratch(d, width):
-    return pltpu.VMEM((3, d.frames, (d.height + 2) * d.line, width), BF)
+    return pltpu.VMEM((d.frames, (d.height + 2) * d.line, 3 * width), BF)
 
 
 def time_scratch(d, width):
@@ -124,20 +131,23 @@
     cells, width = values.shape
     place = lax.broadcasted_iota(jnp.int32, (cells, width), 0)
     column = lax.rem(lax.div(place, d.clips), d.width)
-    edge = jnp.zeros((3, d.frames, d.line, width), BF)
-    pad[:, :, 0 : d.line, :] = edge
-    pad[:, :, d.line + d.plane :, :] = edge
+    edge = jnp.zeros((d.frames, d.line, 3 * width), BF)
+    pad[:, 0 : d.line, :] = edge
+    pad[:, d.line + d.plane :, :] = edge
     left = jnp.where(column > 0, pltpu.roll(values, d.clips, 0), 0.0)
     right = jnp.where(column < d.width - 1, pltpu.roll(values, cells - d.clips, 0), 0.0)
     for j, moved in enumerate((left, values, right)):
-        pad[j, :, d.line : d.line + d.plane, :] = moved.astype(BF).reshape(
-            d.frames, d.plane, width
-        )
-
-
-def space_window(d, pad, i, j):
-    start = pl.multiple_of(i * d.line, d.line)
-    block = pad[j, :, pl.ds(start, d.plane), :]
+        block = moved.astype(BF).reshape(d.frames, d.plane, width)
+        pad[:, d.line : d.line + d.plane, j * width : (j + 1) * width] = block
+
+
+def space_window(d, pad, i, j=None):
+    rows = pl.ds(pl.multiple_of(i * d.line, d.line), d.plane)
+    if j is None:
+        block = pad[:, rows, :]
+    else:
+        width = pad.shape[-1] // 3
+        block = pad[:, rows, pl.ds(pl.multiple_of(j * width, LANES), width)]
     return block.reshape(d.cells, block.shape[-1])
 
 
@@ -162,11 +172,30 @@
     return jnp.concatenate(rows, axis=0)
 
 
+def total_of(d, ids, terms):
+    z = ids[3]
+    values = [term[...] for term in terms]
+    total = None
+    for place in range(d.nz):
+        here = values[0]
+        for k in range(1, d.nz):
+            here = jnp.where(lax.rem(z + (d.nz - k), d.nz) == place, values[k], here)
+        total = here if total is None else total + here
+    return total
+
+
 def coefs_of(total, count, gains):
     average = total[0:1] / count
     scale = lax.rsqrt(total[1:2] / count - average * average + EPS_NORM)
     return jnp.concatenate(
-        [average, scale, gains[0:2], jnp.zeros((4, total.shape[1]), F32)], axis=0
+        [
+            average,
+            scale,
+            gains[0:2],
+            jnp.broadcast_to(count, average.shape),
+            jnp.zeros((3, total.shape[1]), F32),
+        ],
+        axis=0,
     )
 
 
@@ -185,12 +214,10 @@
 
 
 def conv_space_into(d, acc, pad, weight):
-    acc[...] = jnp.zeros_like(acc)
-
-    @pl.loop(0, SPACE)
-    def _(k):
-        window = space_window(d, pad, lax.div(k, 3), lax.rem(k, 3))
-        acc[...] += dot(window, weight[k])
+    for i in range(3):
+        three = weight[3 * i : 3 * i + 3].reshape(3 * d.channels, d.half)
+        part = dot(space_window(d, pad, i), three)
+        acc[...] = part if i == 0 else acc[...] + part
 
 
 def first_space_kernel(d, w, *refs):
@@ -211,10 +238,11 @@
 def second_space_kernel(d, w, *refs):
     ids, *refs = refs
     w_refs, refs = refs[: len(w.arrays)], refs[len(w.arrays) :]
-    q, va, vb, count, gains, mask, a_out, coef_out, s_out, sums_out, weight, sems, pad = refs
+    terms, refs = refs[: d.nz], refs[d.nz :]
+    q, count, gains, mask, a_out, coef_out, s_out, sums_out, weight, sems, pad = refs
     copies = w.start(d, ids, w_refs, weight, sems)
     m = mask[...]
-    coef = coefs_of(va[...] + vb[...], count[...], gains[...])
+    coef = coefs_of(total_of(d, ids, terms), count[4:5, 0:1], gains[...])
     coef_out[...] = coef
     pre = coef[2:3] * normed_of(q[...].astype(F32), coef) + coef[3:4]
     act = jax.nn.silu(pre) * m
@@ -230,9 +258,12 @@
 def time_kernel(d, w, *refs):
     ids, *refs = refs
     w_refs, refs = refs[: len(w.arrays)], refs[len(w.arrays) :]
-    s, va, vb, count, gains, mask, a_out, q_out, coef_out, weight, sems, pad = refs
+    terms, refs = refs[: d.nz], refs[d.nz :]
+    s, *counts, gains, mask, a_out, q_out, coef_out, weight, sems, pad = refs
     copies = w.start(d, ids, w_refs, weight, sems)
-    coef = coefs_of(va[...] + vb[...], count[...], gains[...])
+    total = total_of(d, ids, terms)
+    count = counts[0][4:5, 0:1] if counts else total[2:3, 0:1]
+    coef = coefs_of(total, count, gains[...])
     coef_out[...] = coef
     pre = coef[2:3] * normed_of(s[...], coef) + coef[3:4]
     act = (jax.nn.silu(pre) * mask[...]).astype(BF)
@@ -257,11 +288,12 @@
 def head_kernel(d, w, denominator, classes, *refs):
     ids, *refs = refs
     w_refs, refs = refs[: len(w.arrays)], refs[len(w.arrays) :]
-    q, va, vb, count, gains, mask, x, bias, clip_info, labels, *refs = refs
+    terms, refs = refs[: d.nz], refs[d.nz :]
+    q, count, gains, mask, x, bias, clip_info, labels, *refs = refs
     coef_out, grad_out, sums_out, head, sems = refs
     copies = w.start(d, ids, w_refs, head, sems)
     m = mask[...]
-    coef = coefs_of(va[...] + vb[...], count[...], gains[...])
+    coef = coefs_of(total_of(d, ids, terms), count[4:5, 0:1], gains[...])
     coef_out[...] = coef
     normed = normed_of(q[...].astype(F32), coef)
     pre = coef[2:3] * normed + coef[3:4] + x[...].astype(F32)
@@ -309,15 +341,16 @@
 def time_back_kernel(d, w, *refs):
     ids, *refs = refs
     w_refs, refs = refs[: len(w.arrays)], refs[len(w.arrays) :]
-    grad_two, q, coef_two, va, vb, count, mask, s, coef_one, *refs = refs
+    terms, refs = refs[: d.nz], refs[d.nz :]
+    grad_two, q, coef_two, count, mask, s, coef_one, *refs = refs
     gq_out, grad_out, sums_out, tot_out, weight, sems, pad = refs
     copies = w.start(d, ids, w_refs, weight, sems)
     m = mask[...]
-    total = va[...] + vb[...]
+    total = total_of(d, ids, terms)
     tot_out[...] = total
     coef = coef_two[...]
     normed = normed_of(q[...].astype(F32), coef)
-    grad_q = norm_back(grad_two[...], normed, coef, total, count[...], m).astype(BF)
+    grad_q = norm_back(grad_two[...], normed, coef, total, count[4:5, 0:1], m).astype(BF)
     gq_out[...] = grad_q
     fill_time(d, pad, grad_q)
     for copy in copies:
@@ -337,25 +370,22 @@
 def space_back_kernel(d, w, *refs):
     ids, *refs = refs
     w_refs, refs = refs[: len(w.arrays)], refs[len(w.arrays) :]
-    grad_pre, s, coef_one, va, vb, count, mask, *refs = refs
+    terms, refs = refs[: d.nz], refs[d.nz :]
+    grad_pre, s, coef_one, count, mask, *refs = refs
     gs_out, ga_out, tot_out, weight, sems, pad, acc = refs
     copies = w.start(d, ids, w_refs, weight, sems)
-    total = va[...] + vb[...]
+    total = total_of(d, ids, terms)
     tot_out[...] = total
     coef = coef_one[...]
     normed = normed_of(s[...], coef)
-    grad_s = norm_back(grad_pre[...], normed, coef, total, count[...], mask[...])
+    grad_s = norm_back(grad_pre[...], normed, coef, total, count[4:5, 0:1], mask[...])
     gs_out[...] = grad_s.astype(BF)
     fill_space(d, pad, grad_s)
     for copy in copies:
         copy.wait()
-    acc[...] = jnp.zeros_like(acc)
-
-    @pl.loop(0, SPACE)
-    def _(k):
-        window = space_window(d, pad, 2 - lax.div(k, 3), 2 - lax.rem(k, 3))
-        acc[...] += dot_nt(window, weight[k])
-
+    for i in range(3):
+        part = sum(dot_nt(space_window(d, pad, 2 - i, 2 - j), weight[3 * i + j]) for j in range(3))
+        acc[...] = part if i == 0 else acc[...] + part
     ga_out[...] = acc[...].astype(BF)
 
 
@@ -392,37 +422,60 @@
     write_grad(d, w, ids, dot(turned[...], time_window(d, pad, k)), outs, held)
 
 
-def space_grad_kernel(d, w, *refs):
-    ids, a, grad_s, *refs = refs
-    outs, (pad, turned, held) = refs[:-3], refs[-3:]
+def unit_grad_kernel(d, w, *refs):
+    ids, a, grad_s, grad_q, act, *refs = refs
+    outs, (pad, time_pad, time_turned, turned, held) = refs[:-5], refs[-5:]
     k = pl.program_id(0)
 
     @pl.when(k == 0)
     def _():
         fill_space(d, pad, grad_s[...].astype(F32))
         turned[...] = jnp.transpose(a[...].astype(F32)).astype(BF)
-
-    window = space_window(d, pad, 2 - lax.div(k, 3), 2 - lax.rem(k, 3))
-    write_grad(d, w, ids, dot(turned[...], window), outs, held)
+        fill_time(d, time_pad, act[...])
+        time_turned[...] = jnp.transpose(grad_q[...].astype(F32)).astype(BF)
+
+    @pl.when(k < SPACE)
+    def _():
+        window = space_window(d, pad, 2 - lax.div(k, 3), 2 - lax.rem(k, 3))
+        write_grad(d, w, ids, dot(turned[...], window), outs, held)
+
+    @pl.when(k >= SPACE)
+    def _():
+        window = time_window(d, time_pad, k - SPACE)
+        write_grad(d, w, ids, dot(time_turned[...], window), outs, held)
 
 
 def last_space_grad_kernel(d, w, *refs):
-    ids, a, grad_pre, s, coef_one, va, vb, count, mask, tot_out, *refs = refs
+    ids, *refs = refs
+    terms, refs = refs[: d.nz], refs[d.nz :]
+    a, grad_pre, s, coef_one, count, mask, tot_out, *refs = refs
     outs, (pad, turned, held) = refs[:-3], refs[-3:]
     k = pl.program_id(0)
 
     @pl.when(k == 0)
     def _():
-        total = va[...] + vb[...]
+        total = total_of(d, ids, terms)
         tot_out[...] = total
         coef = coef_one[...]
         normed = normed_of(s[...], coef)
-        grad_s = norm_back(grad_pre[...], normed, coef, total, count[...], mask[...])
+        grad_s = norm_back(grad_pre[...], normed, coef, total, count[4:5, 0:1], mask[...])
         fill_space(d, pad, grad_s)
         turned[...] = jnp.transpose(a[...].astype(F32)).astype(BF)
 
     window = space_window(d, pad, 2 - lax.div(k, 3), 2 - lax.rem(k, 3))
     write_grad(d, w, ids, dot(turned[...], window), outs, held)
+
+
+def squares_kernel(*refs):
+    *values, out = refs
+    row = lax.broadcasted_iota(jnp.int32, (8, LANES), 0)
+    lane = lax.broadcasted_iota(jnp.int32, (8, LANES), 1)
+    total = jnp.zeros((8, LANES), F32)
+    for i, value in enumerate(values):
+        here = (row == i // 5) & (lane == i % 5)
+        lanes = jnp.sum(value[...], axis=0, keepdims=True)
+        total = jnp.where(here, jnp.sum(lanes, axis=1, keepdims=True), total)
+    out[...] = total
 
 
 def sds(shape, dtype=F32):
@@ -443,7 +496,10 @@
 
 
 def w_ins(weight):
-    return [(anywhere(), piece) for piece in weight.arrays]
+    return [
+        (in_hbm(), pltpu.with_memory_space_constraint(piece, pltpu.HBM))
+        for piece in weight.arrays
+    ]
 
 
 def v_ins(*values):
@@ -452,15 +508,18 @@
 
 def grad_call(d, body, name, kind, taps, ids, values, first_outs, scratch):
     if kind == "ring":
-        shape, count = (2, taps, d.rows, d.half), 2 * d.groups
-        spec = pl.BlockSpec((2, 1, d.rows, d.half), lambda k: (0, k, 0, 0))
-    elif kind == "all":
-        shape, count = (d.groups, 2, taps, d.rows, d.half), 2
-        spec = pl.BlockSpec((d.groups, 2, 1, d.rows, d.half), lambda k: (0, 0, k, 0, 0))
+        shape, count = (d.nz, 2, taps, d.rows, d.half), 4
+        spec = pl.BlockSpec((d.nz, 2, 1, d.rows, d.half), lambda k: (0, 0, k, 0, 0))
+    elif kind == "parts":
+        shape, count = (2, 2, taps, d.rows, d.half), d.groups // 2
+        spec = pl.BlockSpec((2, 2, 1, d.rows, d.half), lambda k: (0, 0, k, 0, 0))
+        first_outs = [*first_outs, sds((d.groups, *shape[1:]), BF)]
     else:
         shape, count = (taps, d.channels, d.half), 1
         spec = pl.BlockSpec((1, d.channels, d.half), lambda k: (k, 0, 0))
     fixed = [pl.BlockSpec(out.shape, lambda k: (0, 0)) for out in first_outs]
+    if kind == "parts":
+        fixed[-1] = pl.BlockSpec((d.groups, 2, 1, d.rows, d.half), lambda k: (0, 0, k, 0, 0))
     outs = pl.pallas_call(
         functools.partial(body, d, Weight(kind, (), 0, 1)),
         name=name,
@@ -471,11 +530,7 @@
         scratch_shapes=scratch
         + [pltpu.VMEM((d.channels, d.cells), BF), pltpu.VMEM((d.channels, d.half), BF)],
         compiler_params=pltpu.CompilerParams(vmem_limit_bytes=40 * MB),
-        cost_estimate=pl.CostEstimate(
-            flops=2 * taps * d.cells * d.channels * d.half,
-            bytes_accessed=8 * MB,
-            transcendentals=0,
-        ),
+        cost_estimate=pl.CostEstimate(flops=1, bytes_accessed=1, transcendentals=0),
     )(ids, *values)
     return outs[: len(first_outs)], outs[len(first_outs) :]
 
@@ -485,30 +540,37 @@
     return lax.ppermute(value, axis, [(i, i ^ distance) for i in range(size)])
 
 
-def data_hops():
-    hops = []
-    for axis in DATA:
-        distance = 1
-        while distance < lax.axis_size(axis):
-            hops.append((axis, distance))
-            distance *= 2
-    return hops
-
-
-def data_sums(values):
-    hops = data_hops()
-    for axis, distance in hops[:-1]:
-        values = values + swap(values, axis, distance)
-    return values, swap(values, *hops[-1])
+def across_yy(values, *besides):
+    size = lax.axis_size("yy")
+    distance = 1
+    while distance < size:
+        other = swap(values, "yy", distance)
+        distance *= 2
+        values = values + (after(other, *besides) if distance >= size else other)
+    return values
+
+
+def around_tm(values):
+    size = lax.axis_size("tm")
+    return [values] + [
+        lax.ppermute(values, "tm", [(i, (i + k) % size) for i in range(size)])
+        for k in range(1, size)
+    ]
+
+
+def data_sums(values, last=(), first=()):
+    terms = around_tm(across_yy(values, *first))
+    return [after(term, *last) if k == len(terms) - 1 else term for k, term in enumerate(terms)]
 
 
 def data_sums_gather(values):
-    hops = data_hops()
-    for axis, distance in hops[:-1]:
-        other = swap(values, axis, distance)
+    distance = 1
+    while distance < lax.axis_size("yy"):
+        other = swap(values, "yy", distance)
         values = jnp.concatenate([values[:8] + other[:8], values[8:], other[8:]], axis=0)
-    other = swap(values, *hops[-1])
-    return values[:8], other[:8], jnp.concatenate([values[8:], other[8:]], axis=0)
+        distance *= 2
+    terms = around_tm(values)
+    return [term[:8] for term in terms], jnp.concatenate([term[8:] for term in terms], axis=0)
 
 
 def pick(index, first, second):
@@ -516,6 +578,8 @@
 
 
 def after(value, *earlier):
+    if not earlier:
+        return value
     return lax.optimization_barrier((value, *earlier))[0]
 
 
@@ -524,18 +588,27 @@
     return lax.ppermute(value, "tm", [(i, (i + 1) % size) for i in range(size)])
 
 
-def gather_ring(both):
-    held, across = [both], [swap(both, "yy")]
-    for _ in range(lax.axis_size("tm") - 1):
-        held.append(turn(held[-1]))
-        across.append(swap(held[-1], "yy"))
+def together(*values):
+    return lax.optimization_barrier(values)
+
+
+def gather_ring(both, besides):
+    held, across, made = [both], [], []
+    for beside in besides:
+        moves = [swap(held[-1], "yy")]
+        if len(held) < lax.axis_size("tm"):
+            moves.append(turn(held[-1]))
+        extra = beside(held[-1], made[-1] if made else None)
+        results = together(*moves, *extra)
+        across.append(results[0])
+        held += results[1 : len(moves)]
+        made.append(results[len(moves) :])
     own = held + across
-    return Weight("ring", own + [swap(block, "u") for block in own], 0, both.shape[1])
+    return Weight("blocks", own + [swap(block, "u") for block in own], 0, both.shape[1]), made
 
 
 def gather_all(d, s, u, both, *earlier):
-    own = lax.all_gather(both, DATA, axis=0, tiled=False)
-    own = after(own, *earlier) if earlier else own
+    own = after(lax.all_gather(both, DATA, axis=0, tiled=False), *earlier)
     sibling = swap(own, "u")
     taps = both.shape[1]
     if d.pieces:
@@ -554,34 +627,39 @@
     return total.astype(BF)
 
 
-def reduce_ring(d, outs):
-    n = d.nz
-    keep, send = outs[: d.groups], outs[d.groups :]
+def reduce_ring(d, gradients):
+    def joined(yrel, k, *others):
+        parts = [outs[yrel][k].astype(F32) + outs[2 + yrel][k].astype(F32) for outs in gradients]
+        total = jnp.concatenate(parts, axis=1)
+        for other in others:
+            total = total + other.astype(F32)
+        return total.astype(BF)
+
     moving = None
-    for k in list(range(1, n)) + [0]:
-        across = swap(added(keep[n + k], swap(send[n + k], "u")), "yy")
-        terms = [keep[k], swap(send[k], "u"), across]
+    for k in list(range(1, d.nz)) + [0]:
+        terms = [swap(joined(1, k), "yy")]
         if moving is not None:
             terms.append(turn(moving))
-        moving = added(*terms)
+        moving = joined(0, k, *terms)
     return moving
 
 
-def reduce_all(d, s, u, kind, out_lists):
-    if kind == "all":
-        both = jnp.concatenate(
-            [added(keep, swap(send, "u")) for keep, send in out_lists], axis=2
-        )
+def reduce_all(d, s, u, kind, outs, *earlier):
+    if kind == "parts":
+        keep, *sends = outs
+        theirs = [swap(send, "u") for send in sends]
     else:
-        natural = jnp.concatenate([outs[0] for outs in out_lists], axis=0)
+        (natural,) = outs
         taps = natural.shape[0]
         parts = natural.reshape(taps, d.ny, 2, 2, d.nz, d.rows, d.half)
         parts = parts.transpose(3, 1, 4, 2, 0, 5, 6)
         parts = jnp.where(u == 0, parts, parts[::-1])
         parts = jnp.where(s == 0, parts, parts[:, :, :, ::-1])
         keep, send = parts.reshape(2, d.groups, 2, taps, d.rows, d.half)
-        both = added(keep, swap(send, "u"))
-    return lax.psum_scatter(both, DATA, scatter_dimension=0, tiled=False)
+        theirs = [swap(send, "u")]
+    keep, theirs = after((keep, theirs), *earlier)
+    both = added(keep, jnp.concatenate(theirs, axis=0))
+    return both, lax.psum_scatter(both, DATA, scatter_dimension=0, tiled=False)
 
 
 def own_rows(d, s, mine):
@@ -600,6 +678,10 @@
     return jnp.concatenate(
         [gain[None], shift[None], jnp.zeros((6, gain.shape[0]), F32)], axis=0
     )
+
+
+def square_rows(values):
+    return jnp.sum(values * values, axis=tuple(range(1, values.ndim - 1)))
 
 
 def adam_part(weight, gradient, moment_one, moment_two, decay):
@@ -644,57 +726,75 @@
     denominator = micro * clips * 4 * ny
 
     def prepared(weight, l):
-        moved = weight[:, l].astype(BF).transpose(1, 0, 2)
-        return halves(d, moved)
-
-    head_slot = jnp.pad(head_weight.astype(BF), ((0, 0), (0, d.half - classes)))[None]
-    space_parts = [prepared(spatial_weight, l) for l in range(2)]
-    time_parts = [prepared(temporal_weight, l) for l in range(2)]
+        return halves(d, weight[:, l].astype(BF).transpose(1, 0, 2))
 
     def paired(parts):
         first = jnp.concatenate([part[0] for part in parts], axis=0)
         second = jnp.concatenate([part[1] for part in parts], axis=0)
-        own = pick(s, first, second)
-        return jnp.stack([own, swap(pick(s, second, first), "s")])
-
-    early = paired([space_parts[0], time_parts[0]])
-    late = paired([space_parts[1], time_parts[1], (head_slot, head_slot)])
+        return jnp.stack([pick(s, first, second), swap(pick(s, second, first), "s")])
+
+    def by_index(index, mine, other):
+        return jnp.stack([pick(index, mine, other), pick(index, other, mine)])
+
+    def beside_first(block, _):
+        moved = []
+        for value in (clips_x, jnp.stack([frames, labels]).transpose(1, 0, 2)):
+            kept = pick(u, value[0], value[1])
+            pair = by_index(u, kept, swap(pick(u, value[1], value[0]), "u"))
+            moved.append(by_index(s, pair, swap(pair, "s")))
+        return moved
+
+    def clips_home(four):
+        return lax.all_to_all(four, "tm", split_axis=0, concat_axis=0, tiled=True)
+
+    def beside_second(block, first):
+        weights = after((spatial_weight, temporal_weight, head_weight), block)
+        late = paired([prepared(weights[0], 1)])
+        slot = jnp.pad(weights[2].astype(BF), ((0, 0), (0, d.half - classes)))[None]
+        four = first[0].reshape(nz, clips, height * width, channels)
+        return late, paired([prepared(weights[1], 1), (slot, slot)]), clips_home(four)
+
+    def beside_third(block, _):
+        weights = after((spatial_weight, temporal_weight, head_weight), block)
+        gains, bias = after((affine, head_bias), block)
+        bias_row = jnp.full((1, channels), -1e30, F32).at[0, :classes].set(bias)
+        rows_one, rows_two = [], []
+        for l in range(2):
+            low, high = halves(d, gains[l, :, :mid])
+            mine = pick(s, low, high)
+            rows_one.append(rows_of(mine[0], mine[1]))
+            rows_two.append(rows_of(gains[l, 0, mid:], gains[l, 1, mid:]))
+        squares = [square_rows(weight[:, l]) for weight in weights[:2] for l in range(2)]
+        return [bias_row, *rows_one, *rows_two, *squares, square_rows(weights[2])]
+
+    early = paired([prepared(spatial_weight, 0), prepared(temporal_weight, 0)])
     if d.pieces:
-        early_w = gather_ring(early)
+        early_w, made = gather_ring(
+            early, [beside_first, beside_second, beside_third, lambda *_: []]
+        )
+        first, second, small, _ = made
     else:
         early_w = gather_all(d, s, u, early)
-
-    def by_index(index, mine, other):
-        return jnp.stack([pick(index, mine, other), pick(index, other, mine)])
-
-    kept = pick(u, clips_x[0], clips_x[1])
-    other = swap(pick(u, clips_x[1], clips_x[0]), "u")
-    pair = by_index(u, kept, other)
-    four = by_index(s, pair, swap(pair, "s"))
-    four = four.reshape(nz, clips, height * width, channels)
-    clip_all = lax.all_to_all(four, "tm", split_axis=0, concat_axis=0, tiled=True)
+        first = beside_first(early, None)
+        second, small = beside_second(early, first), beside_third(early, None)
+    info_four = first[1]
+    late, last, clip_all = second
+    bias_row, *small = small
+    gains_one, gains_two, weight_squares = small[:2], small[2:4], small[4:]
+
     x = clip_all.reshape(nz, clips, height * width, channels)
     x = x.transpose(0, 2, 1, 3).reshape(d.cells, channels)
 
-    info = jnp.stack([frames, labels]).transpose(1, 0, 2)
-    kept_info = pick(u, info[0], info[1])
-    pair_info = by_index(u, kept_info, swap(pick(u, info[1], info[0]), "u"))
-    four_info = by_index(s, pair_info, swap(pair_info, "s")).reshape(nz, 2, clips)
-    mine_info = lax.dynamic_index_in_dim(four_info, z, 0, keepdims=False)
+    mine_info = lax.dynamic_index_in_dim(
+        info_four.reshape(nz, 2, clips), z, 0, keepdims=False
+    )
     my_frames, my_labels = mine_info[0], mine_info[1]
     valid = (jnp.arange(nz, dtype=jnp.int32)[:, None] * 8 < my_frames[None, :]).astype(F32)
     mask = jnp.broadcast_to(valid[:, None, :], (nz, height * width, clips)).reshape(d.cells, 1)
     divisor = (my_frames // 8).astype(F32) * (height * width)
     clip_info = jnp.broadcast_to(jnp.tile(divisor, 8 // clips)[:, None], (8, LANES))
     label_rows = jnp.broadcast_to(jnp.tile(my_labels, 8 // clips)[:, None], (8, LANES))
-    bias_row = jnp.full((1, channels), -1e30, F32).at[0, :classes].set(head_bias)
-
-    gains_one, gains_two = [], []
-    for l in range(2):
-        low, high = halves(d, affine[l, :, :mid])
-        mine = pick(s, low, high)
-        gains_one.append(rows_of(mine[0], mine[1]))
-        gains_two.append(rows_of(affine[l, 0, mid:], affine[l, 1, mid:]))
+    x, mask, clip_info, label_rows = together(x, mask, clip_info, label_rows)
 
     wide, narrow = (d.cells, d.half), (d.cells, channels)
     space_flops = 2 * d.cells * SPACE * channels * d.half
@@ -713,21 +813,21 @@
             space_flops,
         )
 
-    def space_next(q, va, vb, count):
+    def space_next(q, terms, count):
         return call(
             functools.partial(second_space_kernel, d, space_w[1]),
             "space1",
-            [(smem(), ids)] + w_ins(space_w[1]) + v_ins(q, va, vb, count, gains_two[0], mask),
+            [(smem(), ids)] + w_ins(space_w[1]) + v_ins(*terms, q, count, gains_two[0], mask),
             [sds(narrow, BF), sds((8, channels)), sds(wide), sds((8, d.half))],
             space_w[1].scratch(d) + [space_scratch(d, channels)],
             space_flops,
         )
 
-    def time_next(l, s_value, va, vb, count):
+    def time_next(l, s_value, terms, *count):
         return call(
             functools.partial(time_kernel, d, time_w[l]),
             f"time{l}",
-            [(smem(), ids)] + w_ins(time_w[l]) + v_ins(s_value, va, vb, count, gains_one[l], mask),
+            [(smem(), ids)] + w_ins(time_w[l]) + v_ins(*terms, s_value, *count, gains_one[l], mask),
             [sds(wide, BF), sds(narrow, BF), sds((8, d.half))],
             time_w[l].scratch(d) + [time_scratch(d, d.half)],
             time_flops,
@@ -744,121 +844,86 @@
         )
 
     s0, sums = space_first(x)
-    va, vb = data_sums(sums)
-    count = va[2:3, 0:1] + vb[2:3, 0:1]
-    late_w = gather_all(d, s, u, late, va)
-    space_w[1] = late_w.part(0, SPACE)
-    time_w[1] = late_w.part(SPACE, TIME)
-    head_w = late_w.part(SPACE + TIME, 1)
-    act0, q_part, coef_one0 = time_next(0, s0, va, vb, count)
+    terms = data_sums(sums)
+    act0, q_part, coef_one0 = time_next(0, s0, terms)
+    count = coef_one0
+    space_w[1] = gather_all(d, s, u, late, q_part)
     q0, sums = joined(q_part)
-    va, vb = data_sums(sums)
-    a_mid, coef_two0, s1, sums = space_next(q0, va, vb, count)
-    va, vb = data_sums(sums)
-    act1, q_part, coef_one1 = time_next(1, s1, va, vb, count)
+    terms = data_sums(sums)
+    a_mid, coef_two0, s1, sums = space_next(q0, terms, count)
+    late_w = gather_all(d, s, u, last, s1)
+    time_w[1] = late_w.part(0, TIME)
+    head_w = late_w.part(TIME, 1)
+    terms = data_sums(sums)
+    act1, q_part, coef_one1 = time_next(1, s1, terms, count)
     q1, sums = joined(q_part)
-    va, vb = data_sums(sums)
+    terms = data_sums(sums)
     coef_two1, grad_two, sums = call(
         functools.partial(head_kernel, d, head_w, float(denominator), classes),
         "head",
         [(smem(), ids)]
         + w_ins(head_w)
-        + v_ins(q1, va, vb, count, gains_two[1], mask, x, bias_row, clip_info, label_rows),
+        + v_ins(*terms, q1, count, gains_two[1], mask, x, bias_row, clip_info, label_rows),
         [sds((8, channels)), sds(narrow), sds((16, channels))],
         head_w.scratch(d),
         4 * d.cells * channels,
     )
-    va, vb, carried = data_sums_gather(sums)
-
-    def time_back(l, grad, q, coef_two, va, vb, s_value, coef_one):
+    terms, carried = data_sums_gather(sums)
+
+    def time_back(l, grad, q, coef_two, terms, s_value, coef_one):
         return call(
             functools.partial(time_back_kernel, d, time_w[l]),
             f"time_back{l}",
             [(smem(), ids)]
             + w_ins(time_w[l])
-            + v_ins(grad, q, coef_two, va, vb, count, mask, s_value, coef_one),
+            + v_ins(*terms, grad, q, coef_two, count, mask, s_value, coef_one),
             [sds(narrow, BF), sds(wide), sds((8, d.half)), sds((8, channels))],
             time_w[l].scratch(d) + [time_scratch(d, channels)],
             time_flops,
         )
 
-    late_kind = "all" if d.pieces else "natural"
+    late_kind = "parts" if d.pieces else "natural"
     early_kind = "ring" if d.pieces else "natural"
 
-    def time_grad(l, grad_q, act):
-        return grad_call(
-            d,
-            time_grad_kernel,
-            f"time_grad{l}",
-            late_kind if l else early_kind,
-            TIME,
-            ids,
-            (grad_q, act),
-            [],
-            [time_scratch(d, d.half)],
-        )[1]
-
     grad_q1, grad_one, sums, tot_two1 = time_back(
-        1, grad_two, q1, coef_two1, va, vb, s1, coef_one1
-    )
-    va, vb = data_sums(sums)
-    time_outs1 = time_grad(1, grad_q1, act1)
+        1, grad_two, q1, coef_two1, terms, s1, coef_one1
+    )
+    terms = data_sums(sums)
     grad_s1, ga_part, tot_one1 = call(
         functools.partial(space_back_kernel, d, space_w[1]),
         "space_back",
-        [(smem(), ids)] + w_ins(space_w[1]) + v_ins(grad_one, s1, coef_one1, va, vb, count, mask),
+        [(smem(), ids)] + w_ins(space_w[1]) + v_ins(*terms, grad_one, s1, coef_one1, count, mask),
         [sds(wide, BF), sds(narrow, BF), sds((8, d.half))],
         space_w[1].scratch(d)
         + [space_scratch(d, d.half), pltpu.VMEM((d.cells, channels), F32)],
         space_flops,
     )
     ga_other = swap(ga_part, "s")
-    _, space_outs1 = grad_call(
+    late_first, late_outs = grad_call(
         d,
-        space_grad_kernel,
-        "space_grad1",
+        unit_grad_kernel,
+        "unit_grad1",
         late_kind,
-        SPACE,
+        SPACE + TIME,
         ids,
-        (a_mid, grad_s1),
+        (a_mid, grad_s1, grad_q1, act1),
         [],
-        [space_scratch(d, d.half)],
-    )
+        [
+            space_scratch(d, d.half),
+            time_scratch(d, d.half),
+            pltpu.VMEM((d.channels, d.cells), BF),
+        ],
+    )
+    late_outs = [*late_first, *late_outs]
     grad_two, sums = call(
         join_back_kernel,
         "join_back",
-        v_ins(ga_part, after(ga_other, *space_outs1), q0, coef_two0, mask),
+        v_ins(ga_part, after(ga_other, *late_outs), q0, coef_two0, mask),
         [sds(narrow), sds((8, channels))],
         [],
-        4 * d.cells * channels,
-    )
-    va, vb = data_sums(sums)
-    grad_q0, grad_one, sums, tot_two0 = time_back(
-        0, grad_two, q0, coef_two0, va, vb, s0, coef_one0
-    )
-    va, vb = data_sums(sums)
-    time_outs0 = time_grad(0, grad_q0, act0)
-    (tot_one0,), space_outs0 = grad_call(
-        d,
-        last_space_grad_kernel,
-        "space_grad0",
-        early_kind,
-        SPACE,
-        ids,
-        (x, grad_one, s0, coef_one0, va, vb, count, mask),
-        [sds((8, d.half))],
-        [space_scratch(d, d.half)],
-    )
-
-    late_sum = reduce_all(d, s, u, late_kind, [space_outs1, time_outs1])
-    late_sum = own_rows(d, s, after(late_sum, *space_outs0))
-    if d.pieces:
-        early_sum = reduce_ring(
-            d, [jnp.concatenate(pair, axis=1) for pair in zip(space_outs0, time_outs0)]
-        )
-    else:
-        early_sum = reduce_all(d, s, u, early_kind, [space_outs0, time_outs0])
-    early_sum = own_rows(d, s, early_sum)
+        20 * 10**9,
+    )
+    late_both, late_sum = reduce_all(d, s, u, late_kind, late_outs, sums)
 
     carried = jnp.concatenate([carried, swap(carried, "u")], axis=0).reshape(-1, 8, channels)
     pooled_all = carried[:, :clips].reshape(-1, channels)
@@ -874,6 +939,55 @@
         (((0,), (0,)), ((), ())),
         preferred_element_type=F32,
     )
+    head_one, head_two, head_dir = adam_part(head_weight, head_grad, head_first, head_second, DECAY)
+    bias_one, bias_two, bias_dir = adam_part(head_bias, bias_grad, bias_first, bias_second, 0.0)
+    head_squares = square_rows(head_dir)
+
+    terms = data_sums(
+        sums,
+        (late_both, head_one, head_two, head_dir, head_squares),
+        (loss_sum, bias_one, bias_two),
+    )
+    grad_q0, grad_one, sums, tot_two0 = time_back(
+        0, grad_two, q0, coef_two0, terms, s0, coef_one0
+    )
+    _, time_outs0 = grad_call(
+        d,
+        time_grad_kernel,
+        "time_grad0",
+        early_kind,
+        TIME,
+        ids,
+        (grad_q0, act0),
+        [],
+        [time_scratch(d, d.half)],
+    )
+    if d.pieces:
+        time_outs0 = [*time_outs0[:2], *(swap(send, "u") for send in time_outs0[2:])]
+    terms = data_sums(sums, time_outs0[2:], time_outs0[:2])
+    (tot_one0,), space_outs0 = grad_call(
+        d,
+        last_space_grad_kernel,
+        "space_grad0",
+        early_kind,
+        SPACE,
+        ids,
+        (*terms, x, grad_one, s0, coef_one0, count, mask),
+        [sds((8, d.half))],
+        [space_scratch(d, d.half)],
+    )
+
+    late_sum = own_rows(d, s, after(late_sum, *space_outs0))
+    if d.pieces:
+        early_sum = reduce_ring(
+            d,
+            [[*space_outs0[:2], *(swap(send, "u") for send in space_outs0[2:])], time_outs0],
+        )
+    else:
+        early_outs = [jnp.concatenate([space_outs0[0], time_outs0[0]], axis=0)]
+        _, early_sum = reduce_all(d, s, u, early_kind, early_outs)
+    early_sum, late_sum = together(early_sum, late_sum)
+    early_sum = own_rows(d, s, early_sum)
 
     ones = jnp.stack([tot_one0[:2], tot_one1[:2]])
     twos = jnp.stack([tot_two0[:2], tot_two1[:2]])
@@ -885,43 +999,44 @@
     both = jnp.concatenate([low, high[..., : mid - d.half], twos], axis=-1)
     affine_grad = jnp.stack([both[:, 1], both[:, 0]], axis=1)
 
-    def step(weight, first, second, gradients):
-        return [
-            (moved[0],) + adam_part(moved[0], gradient, moved[1], moved[2], DECAY)
-            for l, gradient in enumerate(gradients)
-            for moved in [[v[:, l].transpose(1, 0, 2) for v in (weight, first, second)]]
-        ]
-
-    def joined_units(parts):
-        return jnp.stack(parts).transpose(2, 0, 1, 3)
-
-    space_steps = step(
-        spatial_weight, spatial_first, spatial_second, (early_sum[:SPACE], late_sum[:SPACE])
-    )
-    time_steps = step(
-        temporal_weight, temporal_first, temporal_second, (early_sum[SPACE:], late_sum[SPACE:])
-    )
-    head_one, head_two, head_dir = adam_part(head_weight, head_grad, head_first, head_second, DECAY)
+    def units(first, second):
+        return jnp.stack([first, second]).transpose(2, 0, 1, 3)
+
+    spatial_grad = units(early_sum[:SPACE], late_sum[:SPACE])
+    temporal_grad = units(early_sum[SPACE:], late_sum[SPACE:])
+    space_one, space_two, space_dir = adam_part(
+        spatial_weight, spatial_grad, spatial_first, spatial_second, DECAY
+    )
+    time_one, time_two, time_dir = adam_part(
+        temporal_weight, temporal_grad, temporal_first, temporal_second, DECAY
+    )
     affine_one, affine_two, affine_dir = adam_part(
         affine, affine_grad, affine_first, affine_second, 0.0
     )
-    bias_one, bias_two, bias_dir = adam_part(head_bias, bias_grad, bias_first, bias_second, 0.0)
-
-    steps = space_steps + time_steps
-    dir_squares = [jnp.sum(part[3] * part[3]) for part in steps] + [jnp.sum(head_dir * head_dir)]
-    weight_squares = [jnp.sum(part[0] * part[0]) for part in steps]
-    weight_squares.append(jnp.sum(head_weight * head_weight))
-    both_squares = jnp.stack([jnp.stack(weight_squares), jnp.stack(dir_squares)])
-    padded = jnp.pad(both_squares, ((0, 6), (0, LANES - 5)))
+    dir_squares = [square_rows(v[:, l]) for v in (space_dir, time_dir) for l in range(2)]
+    dir_squares.append(head_squares)
+    padded = pl.pallas_call(
+        squares_kernel,
+        name="squares",
+        out_shape=sds((8, LANES)),
+        in_specs=[whole()] * 10,
+        out_specs=whole(),
+    )(*weight_squares, *dir_squares)
+    native = Layout(major_to_minor=(0, 2, 1, 3))
+    moments = [
+        with_layout_constraint(value, native)
+        for value in together(space_one, space_two, time_one, time_two)
+    ]
+    space_one, space_two, time_one, time_two = moments
     padded = padded + swap(padded, "u")
-    padded = padded + swap(padded, "s")
-    padded = sum(data_sums(padded))
+    padded = padded + after(swap(padded, "s"), affine_one, affine_two, affine_dir)
+    terms = data_sums(padded, moments[1:3], (moments[0], moments[3]))
+    terms = jnp.stack(terms)
+    padded = sum(terms[lax.rem(z + (nz - place), nz)] for place in range(nz))
     norms = jnp.sqrt(padded[:2, :5])
     trust = norms[0] / norms[1]
-    new = [part[0] - RATE * trust[i] * part[3] for i, part in enumerate(steps)]
-    space_one, space_two = (joined_units([part[i] for part in space_steps]) for i in (1, 2))
-    time_one, time_two = (joined_units([part[i] for part in time_steps]) for i in (1, 2))
-    new_space, new_time = joined_units(new[:2]), joined_units(new[2:])
+    new_space = spatial_weight - RATE * trust[0:2][None, :, None, None] * space_dir
+    new_time = temporal_weight - RATE * trust[2:4][None, :, None, None] * time_dir
     new_head = head_weight - RATE * trust[4] * head_dir
     new_affine = affine - RATE_SMALL * affine_dir
     new_bias = head_bias - RATE_SMALL * bias_dir

time: 523 us -> 449 us (0.86)
  local copies, waits for them, and re-layouts: 69.2 us -> 24.6 us
  waiting for transfers between devices: 246 us -> 217 us
  other arithmetic: 26.6 us -> 38.3 us
  starting transfers between devices: 82.7 us -> 76 us
    ppermute x6, waiting for transfers between devices: 76.4 us -> 38.6 us  [turn(): return lax.ppermute(value, 'tm', [(i, (i + 1) % size) for i in range(size)])]
    ppermute x70 -> x52, waiting for transfers between devices: 169 us -> 132 us  [swap(): return lax.ppermute(value, axis, [(i, i ^ distance) for i in range(size)])]
    ppermute x0 -> x27, starting transfers between devices: none -> 34.3 us  [around_tm(): lax.ppermute(values, 'tm', [(i, (i + k) % size) for i in range(size)])]
    ppermute x0 -> x27, waiting for transfers between devices: none -> 31.4 us  [around_tm(): lax.ppermute(values, 'tm', [(i, (i + k) % size) for i in range(size)])]
    ppermute x70 -> x52, starting transfers between devices: 65.5 us -> 34.5 us  [swap(): return lax.ppermute(value, axis, [(i, i ^ distance) for i in range(size)])]
    unnamed x197 -> x95, local copies, waits for them, and re-layouts: 40.6 us -> 11.6 us
    all_gather x1 -> x2, waiting for transfers between devices: 0.01 us -> 11.2 us  [gather_all(): own = after(lax.all_gather(both, DATA, axis=0, tiled=False), *earlier)]
    ppermute x6, starting transfers between devices: 12.7 us -> 2.01 us  [turn(): return lax.ppermute(value, 'tm', [(i, (i + 1) % size) for i in range(size)])]
  transfers between devices with their start and end apart: 79 -> 89, of which waited for: 47 -> 62; matrix products, arithmetic and copies ran while one was open for 9% -> 7% of each run, Pallas kernels for 7% -> 10%
where the time goes in v1:
time: 449 us; the launch traced here: 440 us
  waiting for transfers between devices  217 us (48%)
  starting transfers between devices  76 us (17%)
  Pallas kernels  67 us (15%)
  other arithmetic  38.3 us (9%)
  local copies, waits for them, and re-layouts  24.6 us (5%)
  between operations  16.1 us (4%)
    ppermute x52, waiting for transfers between devices, swap(): return lax.ppermute(value, axis, [(i, i ^ distance) for i in range(size)])  132 us
    pallas_call x11, Pallas kernels, call(): pl.pallas_call(body, name=name, out_shape=outs, in_specs=[spec for spec,...  43.5 us
    ppermute x6, waiting for transfers between devices, turn(): return lax.ppermute(value, 'tm', [(i, (i + 1) % size) for i in range(size)])  38.6 us
    ppermute x52, starting transfers between devices, swap(): return lax.ppermute(value, axis, [(i, i ^ distance) for i in range(size)])  34.5 us
    ppermute x27, starting transfers between devices, around_tm(): lax.ppermute(values, 'tm', [(i, (i + k) % size) for i in range(size)])  34.3 us
    ppermute x27, waiting for transfers between devices, around_tm(): lax.ppermute(values, 'tm', [(i, (i + k) % size) for i in range(size)])  31.4 us
    pallas_call x3, Pallas kernels, grad_call(): pl.pallas_call(functools.partial(body, d, Weight(kind, (), 0, 1)), name=n...  21.5 us
    unnamed x95, local copies, waits for them, and re-layouts  11.6 us
  transfers between devices with their start and end apart: 89, of which 62 were waited for; matrix products, arithmetic and copies ran while one was open for 7% of the time, Pallas kernels for 10%

profile of v1, /device:TPU:0, one launch (start us, length us, event | category | flops | bytes accessed | tf_op | source)
XLA Modules:
  0.0 440.0 jit_solution(12805242390556082678)
XLA Ops:
  17.1 4.5 %collective-permute-done.6 = s32[2,2,2]{2,1,0:T(2,128)S(1)} collective-permute-done((s32[2,2,2]{2,1,0:T(2,128)S(1)}, s32[2,2,2]{2,1,0:T(2,128)S(1)}, u32[]{:S(2)}, u32[]{:S(2)}) %collective-permute-start.6) | collective-permute-done | bytes 64 | tf_op jit(solution)/shard_map/ppermute | solution.py:540
  26.8 7.0 %collective-permute-done.1.refs_5_ = bf16[2,12,16,640]{3,2,1,0:T(8,128)(2,1)S(1)} collective-permute-done((bf16[2,12,16,640]{3,2,1,0:T(8,128)(2,1)S(1)}, bf16[2,12,16,640]{3,2,1,0:T(8,128)(2,1)S(1)}, u32[]{:S(2)}, u32[]{:S(2)}) %collective-permute-start.1) | collective-permute-done | bytes 491552 | tf_op jit(solution)/shard_map/ppermute | solution.py:540
  43.2 5.1 %all-to-all-start = ((bf16[4,2,64,512]{3,1,2,0:T(2,128)(2,1)}), bf16[4,2,64,512]{3,1,2,0:T(2,128)(2,1)S(1)}, u32[]{:S(2)}, u32[]{:S(2)}) async-start(bf16[4,2,64,512]{3,1,2,0:T(2,128)(2,1)} %copy.493), calls=%async_computation | async-start | bytes 1048576 | tf_op jit(solution)/shard_map/all_to_all | solution.py:748
  69.6 9.1 %collective-permute-done.11.refs_7_ = bf16[2,12,16,640]{3,2,1,0:T(8,128)(2,1)S(1)} collective-permute-done((bf16[2,12,16,640]{3,2,1,0:T(8,128)(2,1)}, bf16[2,12,16,640]{3,2,1,0:T(8,128)(2,1)S(1)}, u32[]{:S(2)}, u32[]{:S(2)}) %collective-permute-start.11) | collective-permute-done | bytes 491552 | tf_op jit(solution)/shard_map/ppermute | solution.py:540
  78.7 5.7 %collective-permute-done.12.refs_4_ = bf16[2,12,16,640]{3,2,1,0:T(8,128)(2,1)} collective-permute-done((bf16[2,12,16,640]{3,2,1,0:T(8,128)(2,1)}, bf16[2,12,16,640]{3,2,1,0:T(8,128)(2,1)}, u32[]{:S(2)}, u32[]{:S(2)}) %collective-permute-start.12) | collective-permute-done | bytes 491552 | tf_op jit(solution)/shard_map/ppermute | solution.py:588
  86.1 7.4 %collective-permute-done.13.refs_8_ = bf16[2,12,16,640]{3,2,1,0:T(8,128)(2,1)S(1)} collective-permute-done((bf16[2,12,16,640]{3,2,1,0:T(8,128)(2,1)}, bf16[2,12,16,640]{3,2,1,0:T(8,128)(2,1)S(1)}, u32[]{:S(2)}, u32[]{:S(2)}) %collective-permute-start.13) | collective-permute-done | bytes 491552 | tf_op jit(solution)/shard_map/ppermute | solution.py:540
  98.4 7.5 %space0.1 = (f32[512,640]{1,0:T(8,128)S(1)}, f32[8,640]{1,0:T(8,128)S(1)}) custom-call(s32[4]{0:T(128)S(1)} %pad_add_fusion.2.refs_0_, bf16[2,12,16,640]{3,2,1,0:T(8,128)(2,1)} %copy-done.14, bf16[2,12,16,640]{3,2,1,0:T(8,128)(2,1)} %collective-permute-done.2.refs_2_, bf16[2,12,16,640]{3,2,1,0:T(8,128)(2,1)} %collective-permute-done.8.refs_3_, ...), custom_call_target="tpu_custom_call" | custom-call | flops 3019898880 | bytes 8388608 | tf_op jit(solution)/shard_map/space0/pallas_call | solution.py:486
  110.3 4.2 collective-permute-start.25
  126.6 12.6 %collective-permute-done.27.qb = bf16[512,512]{1,0:T(8,128)(2,1)S(1)} collective-permute-done((bf16[512,512]{1,0:T(8,128)(2,1)S(1)}, bf16[512,512]{1,0:T(8,128)(2,1)S(1)}, u32[]{:S(2)}, u32[]{:S(2)}) %collective-permute-start.27) | collective-permute-done | bytes 524320 | tf_op jit(solution)/shard_map/ppermute | solution.py:540
  149.5 7.7 %space1.1 = (bf16[512,512]{1,0:T(8,128)(2,1)S(1)}, f32[8,512]{1,0:T(8,128)S(1)}, f32[512,640]{1,0:T(8,128)S(1)}, f32[8,640]{1,0:T(8,128)S(1)}) custom-call(s32[4]{0:T(128)S(1)} %pad_add_fusion.2.refs_0_, bf16[8,2,9,16,640]{4,3,2,1,0:T(8,128)(2,1)} %bitcast.239, bf16[8,2,9,16,640]{4,3,2,1,0:T(8,128)(2,1)} %collective-permute-done.26.refs_2_, ...), custom_call_target="tpu_custom_call" | custom-call | flops 3019898880 | bytes 8388608 | tf_op jit(solution)/shard_map/space1/pallas_call | solution.py:486
  158.8 8.8 %all-gather.5.cloned.1.call-done = bf16[16,4,16,640]{3,2,1,0:T(8,128)(2,1)} async-done(((bf16[2,4,16,640]{3,2,1,0:T(8,128)(2,1)}), bf16[16,4,16,640]{3,2,1,0:T(8,128)(2,1)}) %all-gather.5.cloned.1.call-update) | async-done | bytes 1310736 | tf_op jit(solution)/shard_map/all_gather | solution.py:611
  184.2 10.2 %collective-permute-done.37.qb = bf16[512,512]{1,0:T(8,128)(2,1)S(1)} collective-permute-done((bf16[512,512]{1,0:T(8,128)(2,1)S(1)}, bf16[512,512]{1,0:T(8,128)(2,1)S(1)}, u32[]{:S(2)}, u32[]{:S(2)}) %collective-permute-start.37) | collective-permute-done | bytes 524320 | tf_op jit(solution)/shard_map/ppermute | solution.py:540
  221.8 4.2 time_back1.1
  237.1 7.5 %space_back.1 = (bf16[512,640]{1,0:T(8,128)(2,1)S(1)}, bf16[512,512]{1,0:T(8,128)(2,1)S(1)}, f32[8,640]{1,0:T(8,128)S(1)}) custom-call(s32[4]{0:T(128)S(1)} %pad_add_fusion.2.refs_0_, bf16[8,2,9,16,640]{4,3,2,1,0:T(8,128)(2,1)} %bitcast.240, bf16[8,2,9,16,640]{4,3,2,1,0:T(8,128)(2,1)} %collective-permute-done.26.refs_2_, f32[8,640]{1,0:T(8,128)S(1)} %add.318.refs_3_, ...), custom_call_target="tpu_custom_call" | custom-call | flops 3019898880 | bytes 8388608 | tf_op jit(solution)/shard_map/space_back/pallas_call | solution.py:486
  246.2 10.4 %unit_grad1.1 = (bf16[8,2,12,16,640]{4,3,2,1,0:T(8,128)(2,1)S(1)}, bf16[2,2,12,16,640]{4,3,2,1,0:T(8,128)(2,1)S(1)}, bf16[2,2,12,16,640]{4,3,2,1,0:T(8,128)(2,1)...) custom-call(s32[4]{0:T(128)S(1)} %pad_add_fusion.2.refs_0_, ...), custom_call_target="tpu_custom_call" | custom-call | flops 1 | bytes 1 | tf_op jit(solution)/shard_map/unit_grad1/pallas_call | solution.py:523
  283.6 4.2 time_back0.1
  305.6 8.1 %space_grad0.1 = (f32[8,640]{1,0:T(8,128)S(1)}, bf16[4,2,9,16,640]{4,3,2,1,0:T(8,128)(2,1)S(1)}, bf16[4,2,9,16,640]{4,3,2,1,0:T(8,128)(2,1)S(1)}, bf16[4,2,9,16,...) custom-call(s32[4]{0:T(128)S(1)} %pad_add_fusion.2.refs_0_, f32[8,640]{1,0:T(8,128)S(1)} %add.332.refs_1_, ...), custom_call_target="tpu_custom_call" | custom-call | flops 1 | bytes 1 | tf_op jit(solution)/shard_map/space_grad0/pallas_call | solution.py:523
  320.1 14.0 %collective-permute-done.71 = bf16[2,12,16,640]{3,2,1,0:T(8,128)(2,1)S(1)} collective-permute-done((bf16[2,12,16,640]{3,2,1,0:T(8,128)(2,1)S(1)}, bf16[2,12,16,640]{3,2,1,0:T(8,128)(2,1)S(1)}, u32[]{:S(2)}, u32[]{:S(2)}) %collective-permute-start.71) | collective-permute-done | bytes 491552 | tf_op jit(solution)/shard_map/ppermute | solution.py:540
  335.5 14.4 %collective-permute-done.70 = bf16[2,12,16,640]{3,2,1,0:T(8,128)(2,1)S(1)} collective-permute-done((bf16[2,12,16,640]{3,2,1,0:T(8,128)(2,1)S(1)}, bf16[2,12,16,640]{3,2,1,0:T(8,128)(2,1)S(1)}, u32[]{:S(2)}, u32[]{:S(2)}) %collective-permute-start.70) | collective-permute-done | bytes 491552 | tf_op jit(solution)/shard_map/ppermute | solution.py:540
  350.0 8.6 %collective-permute-done.72 = bf16[2,12,16,640]{3,2,1,0:T(8,128)(2,1)S(1)} collective-permute-done((bf16[2,12,16,640]{3,2,1,0:T(8,128)(2,1)S(1)}, bf16[2,12,16,640]{3,2,1,0:T(8,128)(2,1)S(1)}, u32[]{:S(2)}, u32[]{:S(2)}) %collective-permute-start.72) | collective-permute-done | bytes 491552 | tf_op jit(solution)/shard_map/ppermute | solution.py:588
  363.6 11.5 %collective-permute-done.73 = bf16[2,12,16,640]{3,2,1,0:T(8,128)(2,1)S(1)} collective-permute-done((bf16[2,12,16,640]{3,2,1,0:T(8,128)(2,1)S(1)}, bf16[2,12,16,640]{3,2,1,0:T(8,128)(2,1)S(1)}, u32[]{:S(2)}, u32[]{:S(2)}) %collective-permute-start.73) | collective-permute-done | bytes 491552 | tf_op jit(solution)/shard_map/ppermute | solution.py:588
  378.9 9.6 %collective-permute-done.74 = bf16[2,12,16,640]{3,2,1,0:T(8,128)(2,1)S(1)} collective-permute-done((bf16[2,12,16,640]{3,2,1,0:T(8,128)(2,1)S(1)}, bf16[2,12,16,640]{3,2,1,0:T(8,128)(2,1)S(1)}, u32[]{:S(2)}, u32[]{:S(2)}) %collective-permute-start.74) | collective-permute-done | bytes 491552 | tf_op jit(solution)/shard_map/ppermute | solution.py:588
  390.3 4.8 %collective-permute-done.76 = bf16[12,16,640]{2,1,0:T(8,128)(2,1)S(1)} collective-permute-done((bf16[12,16,640]{2,1,0:T(8,128)(2,1)S(1)}, bf16[12,16,640]{2,1,0:T(8,128)(2,1)S(1)}, u32[]{:S(2)}, u32[]{:S(2)}) %collective-permute-start.76) | collective-permute-done | bytes 245792 | tf_op jit(solution)/shard_map/ppermute | solution.py:540
  401.9 5.5 %multiply_add_fusion.1 = (f32[16,2,9,1152]{3,1,2,0:T(2,128)S(1)}, f32[16,2,9,1152]{3,1,2,0:T(2,128)}, f32[16,2,9,1152]{3,1,2,0:T(2,128)}) fusion(f32[16,2,9,1152]{3,1,2,0:T(2,128)S(1)} %copy-done.10, f32[1,9,16,1152]{3,0,1,2:T(1,128)S(1)} %copy.508, f32[1,9,16,1152]{3,0,1,2:T(1,128)S(1)} %copy.507, f32[16,2,9,1152]{3,1,2,0:T(2,128)S(1)} %copy-done.20, ...), kind=kLoop, calls=%fused_computation.6 | loop fusion | flops 4313088 | bytes 9289728 | tf_op jit(solution)/shard_map/add | solution.py:691
  (418 shorter events, 231.1 us)
Async XLA Ops:
  15.1 11.6 %collective-permute-start.4 = (bf16[2,2,1,8,8,512]{5,4,3,1,0,2:T(8,128)(2,1)S(1)}, bf16[2,2,1,8,8,512]{5,4,3,1,0,2:T(8,128)(2,1)S(1)}, u32[]{:S(2)}, u32[]{:S(2)}) collective-permute-start(bf16[2,2,1,8,8,512]{5,4,3,1,0,2:T(8,128)(2,1)S(1)} %fusion.20), channel_id=1, source_target_pairs={{0,8},{8,0},{1,9},{9,1},{2,10},{10,2},{3,11},{11,3},{4,12},{12,4},... | collective-permute-start | bytes 786440 | tf_op jit(solution)/shard_map/ppermute | solution.py:540
  21.7 12.2 %collective-permute-start.1 = (bf16[2,12,16,640]{3,2,1,0:T(8,128)(2,1)S(1)}, bf16[2,12,16,640]{3,2,1,0:T(8,128)(2,1)S(1)}, u32[]{:S(2)}, u32[]{:S(2)}) collective-permute-start(bf16[2,12,16,640]{3,2,1,0:T(8,128)(2,1)S(1)} %pad_maximum_fusion.1.refs_1_), channel_id=1, source_target_pairs={{0,16},{16,0},{1,17},{17,1},{2,18},{18,2},{3,19},{19,3},{4,20},{20... | collective-permute-start | bytes 1474568 | tf_op jit(solution)/shard_map/ppermute | solution.py:540
  23.8 13.1 %collective-permute-start.2 = (bf16[2,12,16,640]{3,2,1,0:T(8,128)(2,1)S(1)}, bf16[2,12,16,640]{3,2,1,0:T(8,128)(2,1)}, u32[]{:S(2)}, u32[]{:S(2)}) collective-permute-start(bf16[2,12,16,640]{3,2,1,0:T(8,128)(2,1)S(1)} %pad_maximum_fusion.1.refs_1_), channel_id=1, source_target_pairs={{0,1},{1,2},{2,3},{3,0},{4,5},{5,6},{6,7},{7,4},{8,9},{9,10},{10,1... | collective-permute-start | bytes 1474568 | tf_op jit(solution)/shard_map/ppermute | solution.py:588
  37.7 20.0 %collective-permute-start.7 = (bf16[2,12,16,640]{3,2,1,0:T(8,128)(2,1)}, bf16[2,12,16,640]{3,2,1,0:T(8,128)(2,1)}, u32[]{:S(2)}, u32[]{:S(2)}) collective-permute-start(bf16[2,12,16,640]{3,2,1,0:T(8,128)(2,1)} %collective-permute-done.2.refs_2_), channel_id=1, source_target_pairs={{0,16},{16,0},{1,17},{17,1},{2,18},{18,2},{3,19},{19,3},{4,20},{20... | collective-permute-start | bytes 1474568 | tf_op jit(solution)/shard_map/ppermute | solution.py:540
  38.2 19.5 %collective-permute-start.8 = (bf16[2,12,16,640]{3,2,1,0:T(8,128)(2,1)}, bf16[2,12,16,640]{3,2,1,0:T(8,128)(2,1)}, u32[]{:S(2)}, u32[]{:S(2)}) collective-permute-start(bf16[2,12,16,640]{3,2,1,0:T(8,128)(2,1)} %collective-permute-done.2.refs_2_), channel_id=1, source_target_pairs={{0,1},{1,2},{2,3},{3,0},{4,5},{5,6},{6,7},{7,4},{8,9},{9,10},{10,1... | collective-permute-start | bytes 1474568 | tf_op jit(solution)/shard_map/ppermute | solution.py:588
  39.5 12.1 %collective-permute-start.10 = (bf16[4,16,640]{2,1,0:T(8,128)(2,1)}, bf16[4,16,640]{2,1,0:T(8,128)(2,1)}, u32[]{:S(2)}, u32[]{:S(2)}) collective-permute-start(bf16[4,16,640]{2,1,0:T(8,128)(2,1)} %fusion.30), channel_id=1, source_target_pairs={{0,8},{8,0},{1,9},{9,1},{2,10},{10,2},{3,11},{11,3},{4,12},{12,4},... | collective-permute-start | bytes 245768 | tf_op jit(solution)/shard_map/ppermute | solution.py:540
  43.2 18.4 %all-to-all-start = ((bf16[4,2,64,512]{3,1,2,0:T(2,128)(2,1)}), bf16[4,2,64,512]{3,1,2,0:T(2,128)(2,1)S(1)}, u32[]{:S(2)}, u32[]{:S(2)}) async-start(bf16[4,2,64,512]{3,1,2,0:T(2,128)(2,1)} %copy.493), calls=%async_computation | async-start | bytes 1048576 | tf_op jit(solution)/shard_map/all_to_all | solution.py:748
  48.3 76.2 %all-gather.7.cloned.1.call-start = ((), (), s32[]{:S(2)}) async-start(), calls=%async_computation.4 | async-start | bytes 3317760 | tf_op jit(solution)/shard_map/all_gather | solution.py:611
  61.7 105.9 %all-gather.5.cloned.1.call-start = ((), (), s32[]{:S(2)}) async-start(), calls=%async_computation.3 | async-start | bytes 1474560 | tf_op jit(solution)/shard_map/all_gather | solution.py:611
  62.5 16.2 %collective-permute-start.11 = (bf16[2,12,16,640]{3,2,1,0:T(8,128)(2,1)}, bf16[2,12,16,640]{3,2,1,0:T(8,128)(2,1)S(1)}, u32[]{:S(2)}, u32[]{:S(2)}) collective-permute-start(bf16[2,12,16,640]{3,2,1,0:T(8,128)(2,1)} %collective-permute-done.8.refs_3_), channel_id=1, source_target_pairs={{0,16},{16,0},{1,17},{17,1},{2,18},{18,2},{3,19},{19,3},{4,20},{20... | collective-permute-start | bytes 1474568 | tf_op jit(solution)/shard_map/ppermute | solution.py:540
  63.8 20.6 %collective-permute-start.12 = (bf16[2,12,16,640]{3,2,1,0:T(8,128)(2,1)}, bf16[2,12,16,640]{3,2,1,0:T(8,128)(2,1)}, u32[]{:S(2)}, u32[]{:S(2)}) collective-permute-start(bf16[2,12,16,640]{3,2,1,0:T(8,128)(2,1)} %collective-permute-done.8.refs_3_), channel_id=1, source_target_pairs={{0,1},{1,2},{2,3},{3,0},{4,5},{5,6},{6,7},{7,4},{8,9},{9,10},{10,1... | collective-permute-start | bytes 1474568 | tf_op jit(solution)/shard_map/ppermute | solution.py:588
  124.5 25.0 %collective-permute-start.26 = (bf16[8,2,9,16,640]{4,3,2,1,0:T(8,128)(2,1)}, bf16[8,2,9,16,640]{4,3,2,1,0:T(8,128)(2,1)}, u32[]{:S(2)}, u32[]{:S(2)}) collective-permute-start(bf16[8,2,9,16,640]{4,3,2,1,0:T(8,128)(2,1)} %bitcast.238), channel_id=1, source_target_pairs={{0,4},{4,0},{1,5},{5,1},{2,6},{6,2},{3,7},{7,3},{8,12},{12,8},{9,1... | collective-permute-start | bytes 8847368 | tf_op jit(solution)/shard_map/ppermute | solution.py:540
  124.6 251.7 %reduce-scatter.2.cloned.1.call-start = ((), (), s32[]{:S(2)}) async-start(), calls=%async_computation.2 | async-start | bytes 4423680 | tf_op jit(solution)/shard_map/reduce_scatter | solution.py:662
  124.6 14.6 %collective-permute-start.27 = (bf16[512,512]{1,0:T(8,128)(2,1)S(1)}, bf16[512,512]{1,0:T(8,128)(2,1)S(1)}, u32[]{:S(2)}, u32[]{:S(2)}) collective-permute-start(bf16[512,512]{1,0:T(8,128)(2,1)S(1)} %get-tuple-element.154.qa), channel_id=1, source_target_pairs={{0,8},{8,0},{1,9},{9,1},{2,10},{10,2},{3,11},{11,3},{4,12},{12,4},... | collective-permute-start | bytes 1572872 | tf_op jit(solution)/shard_map/ppermute | solution.py:540
  182.6 11.8 %collective-permute-start.37 = (bf16[512,512]{1,0:T(8,128)(2,1)S(1)}, bf16[512,512]{1,0:T(8,128)(2,1)S(1)}, u32[]{:S(2)}, u32[]{:S(2)}) collective-permute-start(bf16[512,512]{1,0:T(8,128)(2,1)S(1)} %get-tuple-element.164.qa), channel_id=1, source_target_pairs={{0,8},{8,0},{1,9},{9,1},{2,10},{10,2},{3,11},{11,3},{4,12},{12,4},... | collective-permute-start | bytes 1572872 | tf_op jit(solution)/shard_map/ppermute | solution.py:540
  244.6 13.1 %collective-permute-start.51 = (bf16[512,512]{1,0:T(8,128)(2,1)S(1)}, bf16[512,512]{1,0:T(8,128)(2,1)S(1)}, u32[]{:S(2)}, u32[]{:S(2)}) collective-permute-start(bf16[512,512]{1,0:T(8,128)(2,1)S(1)} %get-tuple-element.177.ga), channel_id=1, source_target_pairs={{0,8},{8,0},{1,9},{9,1},{2,10},{10,2},{3,11},{11,3},{4,12},{12,4},... | collective-permute-start | bytes 1572872 | tf_op jit(solution)/shard_map/ppermute | solution.py:540
  317.5 16.7 %collective-permute-start.71 = (bf16[2,12,16,640]{3,2,1,0:T(8,128)(2,1)S(1)}, bf16[2,12,16,640]{3,2,1,0:T(8,128)(2,1)S(1)}, u32[]{:S(2)}, u32[]{:S(2)}) collective-permute-start(bf16[2,12,16,640]{3,2,1,0:T(8,128)(2,1)S(1)} %pad_maximum_fusion.5), channel_id=1, source_target_pairs={{0,16},{16,0},{1,17},{17,1},{2,18},{18,2},{3,19},{19,3},{4,20},{20... | collective-permute-start | bytes 1474568 | tf_op jit(solution)/shard_map/ppermute | solution.py:540
  317.7 32.2 %collective-permute-start.70 = (bf16[2,12,16,640]{3,2,1,0:T(8,128)(2,1)S(1)}, bf16[2,12,16,640]{3,2,1,0:T(8,128)(2,1)S(1)}, u32[]{:S(2)}, u32[]{:S(2)}) collective-permute-start(bf16[2,12,16,640]{3,2,1,0:T(8,128)(2,1)S(1)} %pad_maximum_fusion.4), channel_id=1, source_target_pairs={{0,16},{16,0},{1,17},{17,1},{2,18},{18,2},{3,19},{19,3},{4,20},{20... | collective-permute-start | bytes 1474568 | tf_op jit(solution)/shard_map/ppermute | solution.py:540
  334.3 24.3 %collective-permute-start.72 = (bf16[2,12,16,640]{3,2,1,0:T(8,128)(2,1)S(1)}, bf16[2,12,16,640]{3,2,1,0:T(8,128)(2,1)S(1)}, u32[]{:S(2)}, u32[]{:S(2)}) collective-permute-start(bf16[2,12,16,640]{3,2,1,0:T(8,128)(2,1)S(1)} %fusion.7), channel_id=1, source_target_pairs={{0,1},{1,2},{2,3},{3,0},{4,5},{5,6},{6,7},{7,4},{8,9},{9,10},{10,1... | collective-permute-start | bytes 1474568 | tf_op jit(solution)/shard_map/ppermute | solution.py:588
  334.4 24.5 %collective-permute-start.79 = (f32[2,2,1152]{2,1,0:T(2,128)S(1)}, f32[2,2,1152]{2,1,0:T(2,128)S(1)}, u32[]{:S(2)}, u32[]{:S(2)}) collective-permute-start(f32[2,2,1152]{2,1,0:T(2,128)S(1)} %maximum_maximum_fusion), channel_id=1, source_target_pairs={{0,4},{4,0},{1,5},{5,1},{2,6},{6,2},{3,7},{7,3},{8,12},{12,8},{9,1... | collective-permute-start | bytes 55304 | tf_op jit(solution)/shard_map/ppermute | solution.py:540
  334.5 29.1 %collective-permute-start.69 = (bf16[2,12,16,640]{3,2,1,0:T(8,128)(2,1)S(1)}, bf16[2,12,16,640]{3,2,1,0:T(8,128)(2,1)S(1)}, u32[]{:S(2)}, u32[]{:S(2)}) collective-permute-start(bf16[2,12,16,640]{3,2,1,0:T(8,128)(2,1)S(1)} %pad_maximum_fusion.3), channel_id=1, source_target_pairs={{0,16},{16,0},{1,17},{17,1},{2,18},{18,2},{3,19},{19,3},{4,20},{20... | collective-permute-start | bytes 1474568 | tf_op jit(solution)/shard_map/ppermute | solution.py:540
  358.8 16.3 %collective-permute-start.73 = (bf16[2,12,16,640]{3,2,1,0:T(8,128)(2,1)S(1)}, bf16[2,12,16,640]{3,2,1,0:T(8,128)(2,1)S(1)}, u32[]{:S(2)}, u32[]{:S(2)}) collective-permute-start(bf16[2,12,16,640]{3,2,1,0:T(8,128)(2,1)S(1)} %fusion.6), channel_id=1, source_target_pairs={{0,1},{1,2},{2,3},{3,0},{4,5},{5,6},{6,7},{7,4},{8,9},{9,10},{10,1... | collective-permute-start | bytes 1474568 | tf_op jit(solution)/shard_map/ppermute | solution.py:588
  362.7 16.2 %collective-permute-start.68 = (bf16[2,12,16,640]{3,2,1,0:T(8,128)(2,1)S(1)}, bf16[2,12,16,640]{3,2,1,0:T(8,128)(2,1)S(1)}, u32[]{:S(2)}, u32[]{:S(2)}) collective-permute-start(bf16[2,12,16,640]{3,2,1,0:T(8,128)(2,1)S(1)} %pad_maximum_fusion.2), channel_id=1, source_target_pairs={{0,16},{16,0},{1,17},{17,1},{2,18},{18,2},{3,19},{19,3},{4,20},{20... | collective-permute-start | bytes 1474568 | tf_op jit(solution)/shard_map/ppermute | solution.py:540
  375.3 13.2 %collective-permute-start.74 = (bf16[2,12,16,640]{3,2,1,0:T(8,128)(2,1)S(1)}, bf16[2,12,16,640]{3,2,1,0:T(8,128)(2,1)S(1)}, u32[]{:S(2)}, u32[]{:S(2)}) collective-permute-start(bf16[2,12,16,640]{3,2,1,0:T(8,128)(2,1)S(1)} %fusion.4), channel_id=1, source_target_pairs={{0,1},{1,2},{2,3},{3,0},{4,5},{5,6},{6,7},{7,4},{8,9},{9,10},{10,1... | collective-permute-start | bytes 1474568 | tf_op jit(solution)/shard_map/ppermute | solution.py:588
  (110 other events, 668.8 us)
Sparse Core Ops, SparseCore 0:
  61.8 62.6 all-gather.6
  127.2 40.3 all-gather.4
  266.1 101.4 reduce-scatter.1

commit v2 on v1

--- a/solution.py
+++ b/solution.py
@@ -636,12 +636,15 @@
         return total.astype(BF)
 
     moving = None
-    for k in list(range(1, d.nz)) + [0]:
+    for k in range(1, d.nz):
         terms = [swap(joined(1, k), "yy")]
         if moving is not None:
             terms.append(turn(moving))
         moving = joined(0, k, *terms)
-    return moving
+    across = swap(joined(1, 0), "yy")
+    last = joined(0, 0, across)
+    theirs = added(last[1], turn(moving[1]))
+    return added(last[0], turn(moving[0])), theirs
 
 
 def reduce_all(d, s, u, kind, outs, *earlier):
@@ -662,11 +665,13 @@
     return both, lax.psum_scatter(both, DATA, scatter_dimension=0, tiled=False)
 
 
-def own_rows(d, s, mine):
-    other = swap(mine[1], "s")
-    first = pick(s, mine[0], other)
-    second = pick(s, other, mine[0])
-    return jnp.concatenate([first, second[..., : d.mid - d.half]], axis=-1).astype(F32)
+def own_rows(d, s, mine, theirs):
+    other = swap(theirs, "s")
+    return pick(s, mine, other), pick(s, other, mine)[..., : d.mid - d.half]
+
+
+def whole_rows(halves_of_rows):
+    return jnp.concatenate(halves_of_rows, axis=-1).astype(F32)
 
 
 def halves(d, values):
@@ -728,31 +733,33 @@
     def prepared(weight, l):
         return halves(d, weight[:, l].astype(BF).transpose(1, 0, 2))
 
-    def paired(parts):
+    def paired(parts, *earlier):
         first = jnp.concatenate([part[0] for part in parts], axis=0)
         second = jnp.concatenate([part[1] for part in parts], axis=0)
-        return jnp.stack([pick(s, first, second), swap(pick(s, second, first), "s")])
+        send = after(pick(s, second, first), *earlier)
+        return jnp.stack([pick(s, first, second), swap(send, "s")])
 
     def by_index(index, mine, other):
         return jnp.stack([pick(index, mine, other), pick(index, other, mine)])
 
-    def beside_first(block, _):
-        moved = []
-        for value in (clips_x, jnp.stack([frames, labels]).transpose(1, 0, 2)):
-            kept = pick(u, value[0], value[1])
-            pair = by_index(u, kept, swap(pick(u, value[1], value[0]), "u"))
-            moved.append(by_index(s, pair, swap(pair, "s")))
-        return moved
+    pairs = []
+    for value in (clips_x, jnp.stack([frames, labels]).transpose(1, 0, 2)):
+        kept = pick(u, value[0], value[1])
+        pairs.append(by_index(u, kept, swap(pick(u, value[1], value[0]), "u")))
+    early = paired([prepared(spatial_weight, 0), prepared(temporal_weight, 0)])
+
+    def beside_first(*_):
+        four, info = (by_index(s, pair, swap(pair, "s")) for pair in pairs)
+        return four.reshape(nz, clips, height * width, channels), info
 
     def clips_home(four):
         return lax.all_to_all(four, "tm", split_axis=0, concat_axis=0, tiled=True)
 
     def beside_second(block, first):
         weights = after((spatial_weight, temporal_weight, head_weight), block)
-        late = paired([prepared(weights[0], 1)])
         slot = jnp.pad(weights[2].astype(BF), ((0, 0), (0, d.half - classes)))[None]
-        four = first[0].reshape(nz, clips, height * width, channels)
-        return late, paired([prepared(weights[1], 1), (slot, slot)]), clips_home(four)
+        parts = [prepared(weights[0], 1), prepared(weights[1], 1), (slot, slot)]
+        return [paired(parts), clips_home(first[0])]
 
     def beside_third(block, _):
         weights = after((spatial_weight, temporal_weight, head_weight), block)
@@ -767,18 +774,16 @@
         squares = [square_rows(weight[:, l]) for weight in weights[:2] for l in range(2)]
         return [bias_row, *rows_one, *rows_two, *squares, square_rows(weights[2])]
 
-    early = paired([prepared(spatial_weight, 0), prepared(temporal_weight, 0)])
     if d.pieces:
         early_w, made = gather_ring(
             early, [beside_first, beside_second, beside_third, lambda *_: []]
         )
-        first, second, small, _ = made
+        (_, info_four), (late, clip_all), small, _ = made
     else:
         early_w = gather_all(d, s, u, early)
-        first = beside_first(early, None)
-        second, small = beside_second(early, first), beside_third(early, None)
-    info_four = first[1]
-    late, last, clip_all = second
+        first = beside_first()
+        info_four = first[1]
+        (late, clip_all), small = beside_second(early, first), beside_third(early, None)
     bias_row, *small = small
     gains_one, gains_two, weight_squares = small[:2], small[2:4], small[4:]
 
@@ -847,13 +852,13 @@
     terms = data_sums(sums)
     act0, q_part, coef_one0 = time_next(0, s0, terms)
     count = coef_one0
-    space_w[1] = gather_all(d, s, u, late, q_part)
     q0, sums = joined(q_part)
     terms = data_sums(sums)
+    late_w = gather_all(d, s, u, late, terms[0])
+    space_w[1] = late_w.part(0, SPACE)
+    time_w[1] = late_w.part(SPACE, TIME)
+    head_w = late_w.part(SPACE + TIME, 1)
     a_mid, coef_two0, s1, sums = space_next(q0, terms, count)
-    late_w = gather_all(d, s, u, last, s1)
-    time_w[1] = late_w.part(0, TIME)
-    head_w = late_w.part(TIME, 1)
     terms = data_sums(sums)
     act1, q_part, coef_one1 = time_next(1, s1, terms, count)
     q1, sums = joined(q_part)
@@ -977,7 +982,7 @@
         [space_scratch(d, d.half)],
     )
 
-    late_sum = own_rows(d, s, after(late_sum, *space_outs0))
+    late_sum = own_rows(d, s, *after((late_sum[0], late_sum[1]), *space_outs0))
     if d.pieces:
         early_sum = reduce_ring(
             d,
@@ -986,8 +991,8 @@
     else:
         early_outs = [jnp.concatenate([space_outs0[0], time_outs0[0]], axis=0)]
         _, early_sum = reduce_all(d, s, u, early_kind, early_outs)
-    early_sum, late_sum = together(early_sum, late_sum)
-    early_sum = own_rows(d, s, early_sum)
+    early_sum = whole_rows(own_rows(d, s, after(early_sum[0], *late_sum), early_sum[1]))
+    late_sum = whole_rows(late_sum)
 
     ones = jnp.stack([tot_one0[:2], tot_one1[:2]])
     twos = jnp.stack([tot_two0[:2], tot_two1[:2]])
@@ -1022,11 +1027,11 @@
         in_specs=[whole()] * 10,
         out_specs=whole(),
     )(*weight_squares, *dir_squares)
-    native = Layout(major_to_minor=(0, 2, 1, 3))
-    moments = [
-        with_layout_constraint(value, native)
-        for value in together(space_one, space_two, time_one, time_two)
-    ]
+    native, by_tap = (Layout(major_to_minor=order) for order in ((0, 2, 1, 3), (1, 2, 0, 3)))
+    moments = together(
+        *(with_layout_constraint(v, by_tap) for v in (space_one, space_two, time_one, time_two))
+    )
+    moments = [with_layout_constraint(value, native) for value in moments]
     space_one, space_two, time_one, time_two = moments
     padded = padded + swap(padded, "u")
     padded = padded + after(swap(padded, "s"), affine_one, affine_two, affine_dir)

time: 449 us -> 428 us (0.953)
  waiting for transfers between devices: 217 us -> 198 us
  other arithmetic: 38.3 us -> 24.2 us
  starting transfers between devices: 76 us -> 83.3 us
  local copies, waits for them, and re-layouts: 24.6 us -> 30.7 us
    ppermute x52 -> x50, waiting for transfers between devices: 132 us -> 98.2 us  [swap(): return lax.ppermute(value, axis, [(i, i ^ distance) for i in range(size)])]
    ppermute x6 -> x7, waiting for transfers between devices: 38.6 us -> 56.7 us  [turn(): return lax.ppermute(value, 'tm', [(i, (i + 1) % size) for i in range(size)])]
    ppermute x52 -> x50, starting transfers between devices: 34.5 us -> 48.1 us  [swap(): return lax.ppermute(value, axis, [(i, i ^ distance) for i in range(size)])]
    all_gather x2 -> x1, waiting for transfers between devices: 11.2 us -> 0.01 us  [gather_all(): own = after(lax.all_gather(both, DATA, axis=0, tiled=False), *earlier)]
    optimization_barrier x1 -> x6, local copies, waits for them, and re-layouts: 0.14 us -> 10.7 us  [together(): return lax.optimization_barrier(values)]
    ppermute x27, starting transfers between devices: 34.3 us -> 27.5 us  [around_tm(): lax.ppermute(values, 'tm', [(i, (i + k) % size) for i in range(size)])]
    unnamed x95 -> x73, local copies, waits for them, and re-layouts: 11.6 us -> 12.8 us
  transfers between devices with their start and end apart: 89 -> 87, of which waited for: 62 -> 56; matrix products, arithmetic and copies ran while one was open for 7% -> 8% of each run, Pallas kernels for 10% -> 9%
where the time goes in v2:
time: 428 us; the launch traced here: 420 us
  waiting for transfers between devices  198 us (46%)
  starting transfers between devices  83.3 us (19%)
  Pallas kernels  66.8 us (16%)
  local copies, waits for them, and re-layouts  30.7 us (7%)
  other arithmetic  24.2 us (6%)
  between operations  16.3 us (4%)
    ppermute x50, waiting for transfers between devices, swap(): return lax.ppermute(value, axis, [(i, i ^ distance) for i in range(size)])  98.2 us
    ppermute x7, waiting for transfers between devices, turn(): return lax.ppermute(value, 'tm', [(i, (i + 1) % size) for i in range(size)])  56.7 us
    ppermute x50, starting transfers between devices, swap(): return lax.ppermute(value, axis, [(i, i ^ distance) for i in range(size)])  48.1 us
    pallas_call x11, Pallas kernels, call(): pl.pallas_call(body, name=name, out_shape=outs, in_specs=[spec for spec,...  43.3 us
    ppermute x27, waiting for transfers between devices, around_tm(): lax.ppermute(values, 'tm', [(i, (i + k) % size) for i in range(size)])  35 us
    ppermute x27, starting transfers between devices, around_tm(): lax.ppermute(values, 'tm', [(i, (i + k) % size) for i in range(size)])  27.5 us
    pallas_call x3, Pallas kernels, grad_call(): pl.pallas_call(functools.partial(body, d, Weight(kind, (), 0, 1)), name=n...  21.6 us
    unnamed x73, local copies, waits for them, and re-layouts  12.8 us
  transfers between devices with their start and end apart: 87, of which 56 were waited for; matrix products, arithmetic and copies ran while one was open for 8% of the time, Pallas kernels for 9%

profile of v2, /device:TPU:0, one launch (start us, length us, event | category | flops | bytes accessed | tf_op | source)
XLA Modules:
  0.0 419.8 jit_solution(4585910728194801825)
XLA Ops:
  16.4 4.5 %collective-permute-done.6 = s32[2,2,2]{2,1,0:T(2,128)S(1)} collective-permute-done((s32[2,2,2]{2,1,0:T(2,128)S(1)}, s32[2,2,2]{2,1,0:T(2,128)S(1)}, u32[]{:S(2)}, u32[]{:S(2)}) %collective-permute-start.6) | collective-permute-done | bytes 64 | tf_op jit(solution)/shard_map/ppermute | solution.py:540
  26.0 8.9 %collective-permute-done.2.refs_2_ = bf16[2,12,16,640]{3,2,1,0:T(8,128)(2,1)} collective-permute-done((bf16[2,12,16,640]{3,2,1,0:T(8,128)(2,1)S(1)}, bf16[2,12,16,640]{3,2,1,0:T(8,128)(2,1)}, u32[]{:S(2)}, u32[]{:S(2)}) %collective-permute-start.2) | collective-permute-done | bytes 491552 | tf_op jit(solution)/shard_map/ppermute | solution.py:588
  38.9 4.1 all-to-all-start
  45.0 4.8 %collective-permute-done.9 = bf16[13,16,640]{2,1,0:T(8,128)(2,1)S(1)} collective-permute-done((bf16[13,16,640]{2,1,0:T(8,128)(2,1)S(1)}, bf16[13,16,640]{2,1,0:T(8,128)(2,1)S(1)}, u32[]{:S(2)}, u32[]{:S(2)}) %collective-permute-start.9) | collective-permute-done | bytes 266272 | tf_op jit(solution)/shard_map/ppermute | solution.py:540
  51.5 7.6 %all-to-all-done = bf16[4,2,64,512]{3,1,2,0:T(2,128)(2,1)S(1)} async-done(((bf16[4,2,64,512]{3,1,2,0:T(2,128)(2,1)}), bf16[4,2,64,512]{3,1,2,0:T(2,128)(2,1)S(1)}, u32[]{:S(2)}, u32[]{:S(2)}) %all-to-all-start) | async-done | bytes 524320 | tf_op jit(solution)/shard_map/all_to_all | solution.py:756
  66.2 14.4 %collective-permute-done.11.refs_4_ = bf16[2,12,16,640]{3,2,1,0:T(8,128)(2,1)} collective-permute-done((bf16[2,12,16,640]{3,2,1,0:T(8,128)(2,1)}, bf16[2,12,16,640]{3,2,1,0:T(8,128)(2,1)}, u32[]{:S(2)}, u32[]{:S(2)}) %collective-permute-start.11) | collective-permute-done | bytes 491552 | tf_op jit(solution)/shard_map/ppermute | solution.py:588
  82.9 7.7 %collective-permute-done.12.refs_8_ = bf16[2,12,16,640]{3,2,1,0:T(8,128)(2,1)S(1)} collective-permute-done((bf16[2,12,16,640]{3,2,1,0:T(8,128)(2,1)}, bf16[2,12,16,640]{3,2,1,0:T(8,128)(2,1)S(1)}, u32[]{:S(2)}, u32[]{:S(2)}) %collective-permute-start.12) | collective-permute-done | bytes 491552 | tf_op jit(solution)/shard_map/ppermute | solution.py:540
  96.4 7.5 %space0.1 = (f32[512,640]{1,0:T(8,128)S(1)}, f32[8,640]{1,0:T(8,128)S(1)}) custom-call(s32[4]{0:T(128)S(1)} %pad_add_fusion.2.refs_0_, bf16[2,12,16,640]{3,2,1,0:T(8,128)(2,1)} %copy-done.10, bf16[2,12,16,640]{3,2,1,0:T(8,128)(2,1)} %collective-permute-done.2.refs_2_, bf16[2,12,16,640]{3,2,1,0:T(8,128)(2,1)} %collective-permute-done.8.refs_3_, ...), custom_call_target="tpu_custom_call" | custom-call | flops 3019898880 | bytes 8388608 | tf_op jit(solution)/shard_map/space0/pallas_call | solution.py:486
  112.7 4.7 %collective-permute-done.23.refs_19_ = f32[8,640]{1,0:T(8,128)S(1)} collective-permute-done((f32[8,640]{1,0:T(8,128)S(1)}, f32[8,640]{1,0:T(8,128)S(1)}, u32[]{:S(2)}, u32[]{:S(2)}) %collective-permute-start.23) | collective-permute-done | bytes 20512 | tf_op jit(solution)/shard_map/ppermute | solution.py:556
  123.7 10.0 %collective-permute-done.25.qb = bf16[512,512]{1,0:T(8,128)(2,1)S(1)} collective-permute-done((bf16[512,512]{1,0:T(8,128)(2,1)S(1)}, bf16[512,512]{1,0:T(8,128)(2,1)S(1)}, u32[]{:S(2)}, u32[]{:S(2)}) %collective-permute-start.25) | collective-permute-done | bytes 524320 | tf_op jit(solution)/shard_map/ppermute | solution.py:540
  147.7 7.5 %space1.1 = (bf16[512,512]{1,0:T(8,128)(2,1)S(1)}, f32[8,512]{1,0:T(8,128)S(1)}, f32[512,640]{1,0:T(8,128)S(1)}, f32[8,640]{1,0:T(8,128)S(1)}) custom-call(s32[4]{0:T(128)S(1)} %pad_add_fusion.2.refs_0_, bf16[8,2,13,16,640]{4,3,2,1,0:T(8,128)(2,1)} %bitcast.215, bf16[8,2,13,16,640]{4,3,2,1,0:T(8,128)(2,1)} %copy-done.5, f32[8,512]{1,0:T(8,128)S(1)} %add.317.refs_3_, ...), custom_call_target="tpu_custom_call" | custom-call | flops 3019898880 | bytes 8388608 | tf_op jit(solution)/shard_map/space1/pallas_call | solution.py:486
  171.9 10.0 %collective-permute-done.35.qb = bf16[512,512]{1,0:T(8,128)(2,1)S(1)} collective-permute-done((bf16[512,512]{1,0:T(8,128)(2,1)S(1)}, bf16[512,512]{1,0:T(8,128)(2,1)S(1)}, u32[]{:S(2)}, u32[]{:S(2)}) %collective-permute-start.35) | collective-permute-done | bytes 524320 | tf_op jit(solution)/shard_map/ppermute | solution.py:540
  208.2 4.1 time_back1.1
  223.1 7.5 %space_back.1 = (bf16[512,640]{1,0:T(8,128)(2,1)S(1)}, bf16[512,512]{1,0:T(8,128)(2,1)S(1)}, f32[8,640]{1,0:T(8,128)S(1)}) custom-call(s32[4]{0:T(128)S(1)} %pad_add_fusion.2.refs_0_, bf16[8,2,13,16,640]{4,3,2,1,0:T(8,128)(2,1)} %bitcast.219, bf16[8,2,13,16,640]{4,3,2,1,0:T(8,128)(2,1)} %copy-done.5, f32[8,640]{1,0:T(8,128)S(1)} %add.321.refs_3_, ...), custom_call_target="tpu_custom_call" | custom-call | flops 3019898880 | bytes 8388608 | tf_op jit(solution)/shard_map/space_back/pallas_call | solution.py:486
  232.1 10.4 %unit_grad1.1 = (bf16[8,2,12,16,640]{4,3,2,1,0:T(8,128)(2,1)S(1)}, bf16[2,2,12,16,640]{4,3,2,1,0:T(8,128)(2,1)S(1)}, bf16[2,2,12,16,640]{4,3,2,1,0:T(8,128)(2,1)...) custom-call(s32[4]{0:T(128)S(1)} %pad_add_fusion.2.refs_0_, ...), custom_call_target="tpu_custom_call" | custom-call | flops 1 | bytes 1 | tf_op jit(solution)/shard_map/unit_grad1/pallas_call | solution.py:523
  270.3 4.2 %time_back0.1 = (bf16[512,512]{1,0:T(8,128)(2,1)S(1)}, f32[512,640]{1,0:T(8,128)S(1)}, f32[8,640]{1,0:T(8,128)S(1)}, f32[8,512]{1,0:T(8,128)S(1)}) custom-call(s32[4]{0:T(128)S(1)} %pad_add_fusion.2.refs_0_, bf16[2,12,16,640]{3,2,1,0:T(8,128)(2,1)} %copy-done.10, bf16[2,12,16,640]{3,2,1,0:T(8,128)(2,1)} %collective-permute-done.2.refs_2_, ...), custom_call_target="tpu_custom_call" | custom-call | flops 1006632960 | bytes 8388608 | tf_op jit(solution)/shard_map/time_back0/pallas_call | solution.py:486
  286.6 4.0 collective-permute-done.60.refs_3_
  290.6 8.1 %space_grad0.1 = (f32[8,640]{1,0:T(8,128)S(1)}, bf16[4,2,9,16,640]{4,3,2,1,0:T(8,128)(2,1)S(1)}, bf16[4,2,9,16,640]{4,3,2,1,0:T(8,128)(2,1)S(1)}, bf16[4,2,9,16,...) custom-call(s32[4]{0:T(128)S(1)} %pad_add_fusion.2.refs_0_, f32[8,640]{1,0:T(8,128)S(1)} %add.335.refs_1_, ...), custom_call_target="tpu_custom_call" | custom-call | flops 1 | bytes 1 | tf_op jit(solution)/shard_map/space_grad0/pallas_call | solution.py:523
  305.1 14.8 %collective-permute-done.69 = bf16[2,12,16,640]{3,2,1,0:T(8,128)(2,1)S(1)} collective-permute-done((bf16[2,12,16,640]{3,2,1,0:T(8,128)(2,1)S(1)}, bf16[2,12,16,640]{3,2,1,0:T(8,128)(2,1)S(1)}, u32[]{:S(2)}, u32[]{:S(2)}) %collective-permute-start.69) | collective-permute-done | bytes 491552 | tf_op jit(solution)/shard_map/ppermute | solution.py:540
  325.5 8.6 %collective-permute-done.68 = bf16[2,12,16,640]{3,2,1,0:T(8,128)(2,1)S(1)} collective-permute-done((bf16[2,12,16,640]{3,2,1,0:T(8,128)(2,1)S(1)}, bf16[2,12,16,640]{3,2,1,0:T(8,128)(2,1)S(1)}, u32[]{:S(2)}, u32[]{:S(2)}) %collective-permute-start.68) | collective-permute-done | bytes 491552 | tf_op jit(solution)/shard_map/ppermute | solution.py:540
  334.2 7.7 %collective-permute-done.70 = bf16[2,12,16,640]{3,2,1,0:T(8,128)(2,1)S(1)} collective-permute-done((bf16[2,12,16,640]{3,2,1,0:T(8,128)(2,1)S(1)}, bf16[2,12,16,640]{3,2,1,0:T(8,128)(2,1)S(1)}, u32[]{:S(2)}, u32[]{:S(2)}) %collective-permute-start.70) | collective-permute-done | bytes 491552 | tf_op jit(solution)/shard_map/ppermute | solution.py:588
  346.2 14.8 %collective-permute-done.71 = bf16[2,12,16,640]{3,2,1,0:T(8,128)(2,1)S(1)} collective-permute-done((bf16[2,12,16,640]{3,2,1,0:T(8,128)(2,1)S(1)}, bf16[2,12,16,640]{3,2,1,0:T(8,128)(2,1)S(1)}, u32[]{:S(2)}, u32[]{:S(2)}) %collective-permute-start.71) | collective-permute-done | bytes 491552 | tf_op jit(solution)/shard_map/ppermute | solution.py:588
  364.0 7.6 %collective-permute-done.74 = bf16[12,16,640]{2,1,0:T(8,128)(2,1)S(1)} collective-permute-done((bf16[12,16,640]{2,1,0:T(8,128)(2,1)S(1)}, bf16[12,16,640]{2,1,0:T(8,128)(2,1)S(1)}, u32[]{:S(2)}, u32[]{:S(2)}) %collective-permute-start.74) | collective-permute-done | bytes 245792 | tf_op jit(solution)/shard_map/ppermute | solution.py:588
  376.0 4.7 %collective-permute-done.75 = bf16[12,16,640]{2,1,0:T(8,128)(2,1)S(1)} collective-permute-done((bf16[12,16,640]{2,1,0:T(8,128)(2,1)S(1)}, bf16[12,16,640]{2,1,0:T(8,128)(2,1)S(1)}, u32[]{:S(2)}, u32[]{:S(2)}) %collective-permute-start.75) | collective-permute-done | bytes 245792 | tf_op jit(solution)/shard_map/ppermute | solution.py:540
  (392 shorter events, 215.2 us)
Async XLA Ops:
  14.3 11.5 %collective-permute-start.4 = (bf16[2,2,1,8,8,512]{5,4,3,1,0,2:T(8,128)(2,1)S(1)}, bf16[2,2,1,8,8,512]{5,4,3,1,0,2:T(8,128)(2,1)S(1)}, u32[]{:S(2)}, u32[]{:S(2)}) collective-permute-start(bf16[2,2,1,8,8,512]{5,4,3,1,0,2:T(8,128)(2,1)S(1)} %fusion.23), channel_id=1, source_target_pairs={{0,8},{8,0},{1,9},{9,1},{2,10},{10,2},{3,11},{11,3},{4,12},{12,4},... | collective-permute-start | bytes 786440 | tf_op jit(solution)/shard_map/ppermute | solution.py:540
  21.0 14.0 %collective-permute-start.2 = (bf16[2,12,16,640]{3,2,1,0:T(8,128)(2,1)S(1)}, bf16[2,12,16,640]{3,2,1,0:T(8,128)(2,1)}, u32[]{:S(2)}, u32[]{:S(2)}) collective-permute-start(bf16[2,12,16,640]{3,2,1,0:T(8,128)(2,1)S(1)} %pad_maximum_fusion.2.refs_1_), channel_id=1, source_target_pairs={{0,1},{1,2},{2,3},{3,0},{4,5},{5,6},{6,7},{7,4},{8,9},{9,10},{10,1... | collective-permute-start | bytes 1474568 | tf_op jit(solution)/shard_map/ppermute | solution.py:588
  23.2 11.8 %collective-permute-start.1 = (bf16[2,12,16,640]{3,2,1,0:T(8,128)(2,1)S(1)}, bf16[2,12,16,640]{3,2,1,0:T(8,128)(2,1)}, u32[]{:S(2)}, u32[]{:S(2)}) collective-permute-start(bf16[2,12,16,640]{3,2,1,0:T(8,128)(2,1)S(1)} %pad_maximum_fusion.2.refs_1_), channel_id=1, source_target_pairs={{0,16},{16,0},{1,17},{17,1},{2,18},{18,2},{3,19},{19,3},{4,20},{20... | collective-permute-start | bytes 1474568 | tf_op jit(solution)/shard_map/ppermute | solution.py:540
  35.0 16.4 %collective-permute-start.8 = (bf16[2,12,16,640]{3,2,1,0:T(8,128)(2,1)}, bf16[2,12,16,640]{3,2,1,0:T(8,128)(2,1)}, u32[]{:S(2)}, u32[]{:S(2)}) collective-permute-start(bf16[2,12,16,640]{3,2,1,0:T(8,128)(2,1)} %collective-permute-done.2.refs_2_), channel_id=1, source_target_pairs={{0,1},{1,2},{2,3},{3,0},{4,5},{5,6},{6,7},{7,4},{8,9},{9,10},{10,1... | collective-permute-start | bytes 1474568 | tf_op jit(solution)/shard_map/ppermute | solution.py:588
  36.1 15.4 %collective-permute-start.7 = (bf16[2,12,16,640]{3,2,1,0:T(8,128)(2,1)}, bf16[2,12,16,640]{3,2,1,0:T(8,128)(2,1)}, u32[]{:S(2)}, u32[]{:S(2)}) collective-permute-start(bf16[2,12,16,640]{3,2,1,0:T(8,128)(2,1)} %collective-permute-done.2.refs_2_), channel_id=1, source_target_pairs={{0,16},{16,0},{1,17},{17,1},{2,18},{18,2},{3,19},{19,3},{4,20},{20... | collective-permute-start | bytes 1474568 | tf_op jit(solution)/shard_map/ppermute | solution.py:540
  38.9 20.1 %all-to-all-start = ((bf16[4,2,64,512]{3,1,2,0:T(2,128)(2,1)}), bf16[4,2,64,512]{3,1,2,0:T(2,128)(2,1)S(1)}, u32[]{:S(2)}, u32[]{:S(2)}) async-start(bf16[4,2,64,512]{3,1,2,0:T(2,128)(2,1)} %copy.118), calls=%async_computation | async-start | bytes 1048576 | tf_op jit(solution)/shard_map/all_to_all | solution.py:756
  43.0 94.9 %all-gather.3.cloned.1.call-start = ((), (), s32[]{:S(2)}) async-start(), calls=%async_computation.3 | async-start | bytes 4792320 | tf_op jit(solution)/shard_map/all_gather | solution.py:611
  59.1 302.4 %reduce-scatter.2.cloned.1.call-start = ((), (), s32[]{:S(2)}) async-start(), calls=%async_computation.2 | async-start | bytes 4423680 | tf_op jit(solution)/shard_map/reduce_scatter | solution.py:665
  59.9 20.7 %collective-permute-start.11 = (bf16[2,12,16,640]{3,2,1,0:T(8,128)(2,1)}, bf16[2,12,16,640]{3,2,1,0:T(8,128)(2,1)}, u32[]{:S(2)}, u32[]{:S(2)}) collective-permute-start(bf16[2,12,16,640]{3,2,1,0:T(8,128)(2,1)} %collective-permute-done.8.refs_3_), channel_id=1, source_target_pairs={{0,1},{1,2},{2,3},{3,0},{4,5},{5,6},{6,7},{7,4},{8,9},{9,10},{10,1... | collective-permute-start | bytes 1474568 | tf_op jit(solution)/shard_map/ppermute | solution.py:588
  59.9 20.7 %collective-permute-start.10 = (bf16[2,12,16,640]{3,2,1,0:T(8,128)(2,1)}, bf16[2,12,16,640]{3,2,1,0:T(8,128)(2,1)S(1)}, u32[]{:S(2)}, u32[]{:S(2)}) collective-permute-start(bf16[2,12,16,640]{3,2,1,0:T(8,128)(2,1)} %collective-permute-done.8.refs_3_), channel_id=1, source_target_pairs={{0,16},{16,0},{1,17},{17,1},{2,18},{18,2},{3,19},{19,3},{4,20},{20... | collective-permute-start | bytes 1474568 | tf_op jit(solution)/shard_map/ppermute | solution.py:540
  82.5 10.4 %collective-permute-start.15 = (bf16[2,12,16,640]{3,2,1,0:T(8,128)(2,1)}, bf16[2,12,16,640]{3,2,1,0:T(8,128)(2,1)}, u32[]{:S(2)}, u32[]{:S(2)}) collective-permute-start(bf16[2,12,16,640]{3,2,1,0:T(8,128)(2,1)} %collective-permute-done.8.refs_3_), channel_id=1, source_target_pairs={{0,4},{4,0},{1,5},{5,1},{2,6},{6,2},{3,7},{7,3},{8,12},{12,8},{9,1... | collective-permute-start | bytes 1474568 | tf_op jit(solution)/shard_map/ppermute | solution.py:540
  122.2 11.5 %collective-permute-start.25 = (bf16[512,512]{1,0:T(8,128)(2,1)S(1)}, bf16[512,512]{1,0:T(8,128)(2,1)S(1)}, u32[]{:S(2)}, u32[]{:S(2)}) collective-permute-start(bf16[512,512]{1,0:T(8,128)(2,1)S(1)} %get-tuple-element.151.qa), channel_id=1, source_target_pairs={{0,8},{8,0},{1,9},{9,1},{2,10},{10,2},{3,11},{11,3},{4,12},{12,4},... | collective-permute-start | bytes 1572872 | tf_op jit(solution)/shard_map/ppermute | solution.py:540
  170.3 11.5 %collective-permute-start.35 = (bf16[512,512]{1,0:T(8,128)(2,1)S(1)}, bf16[512,512]{1,0:T(8,128)(2,1)S(1)}, u32[]{:S(2)}, u32[]{:S(2)}) collective-permute-start(bf16[512,512]{1,0:T(8,128)(2,1)S(1)} %get-tuple-element.160.qa), channel_id=1, source_target_pairs={{0,8},{8,0},{1,9},{9,1},{2,10},{10,2},{3,11},{11,3},{4,12},{12,4},... | collective-permute-start | bytes 1572872 | tf_op jit(solution)/shard_map/ppermute | solution.py:540
  230.6 13.1 %collective-permute-start.49 = (bf16[512,512]{1,0:T(8,128)(2,1)S(1)}, bf16[512,512]{1,0:T(8,128)(2,1)S(1)}, u32[]{:S(2)}, u32[]{:S(2)}) collective-permute-start(bf16[512,512]{1,0:T(8,128)(2,1)S(1)} %get-tuple-element.173.ga), channel_id=1, source_target_pairs={{0,8},{8,0},{1,9},{9,1},{2,10},{10,2},{3,11},{11,3},{4,12},{12,4},... | collective-permute-start | bytes 1572872 | tf_op jit(solution)/shard_map/ppermute | solution.py:540
  299.4 20.7 %collective-permute-start.78 = (f32[2,2,1152]{2,1,0:T(2,128)S(1)}, f32[2,2,1152]{2,1,0:T(2,128)S(1)}, u32[]{:S(2)}, u32[]{:S(2)}) collective-permute-start(f32[2,2,1152]{2,1,0:T(2,128)S(1)} %maximum_maximum_fusion), channel_id=1, source_target_pairs={{0,4},{4,0},{1,5},{5,1},{2,6},{6,2},{3,7},{7,3},{8,12},{12,8},{9,1... | collective-permute-start | bytes 55304 | tf_op jit(solution)/shard_map/ppermute | solution.py:540
  302.4 17.4 %collective-permute-start.69 = (bf16[2,12,16,640]{3,2,1,0:T(8,128)(2,1)S(1)}, bf16[2,12,16,640]{3,2,1,0:T(8,128)(2,1)S(1)}, u32[]{:S(2)}, u32[]{:S(2)}) collective-permute-start(bf16[2,12,16,640]{3,2,1,0:T(8,128)(2,1)S(1)} %pad_maximum_fusion.6), channel_id=1, source_target_pairs={{0,16},{16,0},{1,17},{17,1},{2,18},{18,2},{3,19},{19,3},{4,20},{20... | collective-permute-start | bytes 1474568 | tf_op jit(solution)/shard_map/ppermute | solution.py:540
  304.2 30.0 %collective-permute-start.68 = (bf16[2,12,16,640]{3,2,1,0:T(8,128)(2,1)S(1)}, bf16[2,12,16,640]{3,2,1,0:T(8,128)(2,1)S(1)}, u32[]{:S(2)}, u32[]{:S(2)}) collective-permute-start(bf16[2,12,16,640]{3,2,1,0:T(8,128)(2,1)S(1)} %pad_maximum_fusion.5), channel_id=1, source_target_pairs={{0,16},{16,0},{1,17},{17,1},{2,18},{18,2},{3,19},{19,3},{4,20},{20... | collective-permute-start | bytes 1474568 | tf_op jit(solution)/shard_map/ppermute | solution.py:540
  320.0 21.9 %collective-permute-start.70 = (bf16[2,12,16,640]{3,2,1,0:T(8,128)(2,1)S(1)}, bf16[2,12,16,640]{3,2,1,0:T(8,128)(2,1)S(1)}, u32[]{:S(2)}, u32[]{:S(2)}) collective-permute-start(bf16[2,12,16,640]{3,2,1,0:T(8,128)(2,1)S(1)} %fusion.6), channel_id=1, source_target_pairs={{0,1},{1,2},{2,3},{3,0},{4,5},{5,6},{6,7},{7,4},{8,9},{9,10},{10,1... | collective-permute-start | bytes 1474568 | tf_op jit(solution)/shard_map/ppermute | solution.py:588
  323.9 22.3 %collective-permute-start.67 = (bf16[2,12,16,640]{3,2,1,0:T(8,128)(2,1)S(1)}, bf16[2,12,16,640]{3,2,1,0:T(8,128)(2,1)S(1)}, u32[]{:S(2)}, u32[]{:S(2)}) collective-permute-start(bf16[2,12,16,640]{3,2,1,0:T(8,128)(2,1)S(1)} %pad_maximum_fusion.4), channel_id=1, source_target_pairs={{0,16},{16,0},{1,17},{17,1},{2,18},{18,2},{3,19},{19,3},{4,20},{20... | collective-permute-start | bytes 1474568 | tf_op jit(solution)/shard_map/ppermute | solution.py:540
  342.0 19.0 %collective-permute-start.71 = (bf16[2,12,16,640]{3,2,1,0:T(8,128)(2,1)S(1)}, bf16[2,12,16,640]{3,2,1,0:T(8,128)(2,1)S(1)}, u32[]{:S(2)}, u32[]{:S(2)}) collective-permute-start(bf16[2,12,16,640]{3,2,1,0:T(8,128)(2,1)S(1)} %fusion.5), channel_id=1, source_target_pairs={{0,1},{1,2},{2,3},{3,0},{4,5},{5,6},{6,7},{7,4},{8,9},{9,10},{10,1... | collective-permute-start | bytes 1474568 | tf_op jit(solution)/shard_map/ppermute | solution.py:588
  342.8 18.6 %collective-permute-start.66 = (bf16[2,12,16,640]{3,2,1,0:T(8,128)(2,1)S(1)}, bf16[2,12,16,640]{3,2,1,0:T(8,128)(2,1)S(1)}, u32[]{:S(2)}, u32[]{:S(2)}) collective-permute-start(bf16[2,12,16,640]{3,2,1,0:T(8,128)(2,1)S(1)} %pad_maximum_fusion.3), channel_id=1, source_target_pairs={{0,16},{16,0},{1,17},{17,1},{2,18},{18,2},{3,19},{19,3},{4,20},{20... | collective-permute-start | bytes 1474568 | tf_op jit(solution)/shard_map/ppermute | solution.py:540
  361.2 10.4 %collective-permute-start.74 = (bf16[12,16,640]{2,1,0:T(8,128)(2,1)S(1)}, bf16[12,16,640]{2,1,0:T(8,128)(2,1)S(1)}, u32[]{:S(2)}, u32[]{:S(2)}) collective-permute-start(bf16[12,16,640]{2,1,0:T(8,128)(2,1)S(1)} %get-tuple-element.323), channel_id=1, source_target_pairs={{0,1},{1,2},{2,3},{3,0},{4,5},{5,6},{6,7},{7,4},{8,9},{9,10},{10,1... | collective-permute-start | bytes 737288 | tf_op jit(solution)/shard_map/ppermute | solution.py:588
  361.3 13.0 %collective-permute-start.72 = (bf16[12,16,640]{2,1,0:T(8,128)(2,1)S(1)}, bf16[12,16,640]{2,1,0:T(8,128)(2,1)S(1)}, u32[]{:S(2)}, u32[]{:S(2)}) collective-permute-start(bf16[12,16,640]{2,1,0:T(8,128)(2,1)S(1)} %get-tuple-element.324), channel_id=1, source_target_pairs={{0,1},{1,2},{2,3},{3,0},{4,5},{5,6},{6,7},{7,4},{8,9},{9,10},{10,1... | collective-permute-start | bytes 737288 | tf_op jit(solution)/shard_map/ppermute | solution.py:588
  362.6 13.2 %collective-permute-start.73 = (bf16[12,16,640]{2,1,0:T(8,128)(2,1)S(1)}, bf16[12,16,640]{2,1,0:T(8,128)(2,1)S(1)}, u32[]{:S(2)}, u32[]{:S(2)}) collective-permute-start(bf16[12,16,640]{2,1,0:T(8,128)(2,1)S(1)} %get-tuple-element.209), channel_id=1, source_target_pairs={{0,8},{8,0},{1,9},{9,1},{2,10},{10,2},{3,11},{11,3},{4,12},{12,4},... | collective-permute-start | bytes 737288 | tf_op jit(solution)/shard_map/ppermute | solution.py:540
  (96 other events, 579.7 us)
Sparse Core Ops, SparseCore 0:
  59.2 77.4 all-gather.2
  252.0 105.3 reduce-scatter.1
